TPU v7x, 32 devices: a whole 2x2x4 slice. The times are simulated.
32 devices in a mesh: section: 4 (over z), expert: 8 (over y, x, core).
Axes of the slice: x: 2, y: 2, z: 4, core: 2. Of those that a mesh axis runs over, the one named last changes fastest.
Arguments:
- out_grad: bfloat16 [4, 1024, 2560], P('section', 'expert'), may hold values from -6 to 6
- expert_ids: int32 [4, 1024], P('section', 'expert'), may hold values from 0 to 3, as said below
- slot_ids: int32 [4, 1024], P('section', 'expert'), may hold values from 0 to 32, as said below
- router_logits: float32 [4, 1024, 4], P('section', 'expert'), may hold values from -8 to 8
- saved_routed: bfloat16 [4, 8, 264, 4096], P('section', 'expert'), may hold values from -6 to 6
- w_gate_up: bfloat16 [4, 8, 2560, 4096], P('section', 'expert'), may hold values from -0.125 to 0.125
- w_down: bfloat16 [4, 8, 2048, 2560], P('section', 'expert'), may hold values from -0.09375 to 0.09375
- w_router: bfloat16 [4, 2560, 4], P('section'), may hold values from -0.125 to 0.125
Outputs:
- prev_grad: bfloat16 [4, 1024, 2560], P('section', 'expert')
- routed_hgrad: bfloat16 [4, 8, 264, 4096], P('section', 'expert')
Inputs may be any that keep to these rules, and one draw needn't show every extreme that they name: `expert_ids`: in each aligned block of 128 tokens of a section (one device's), one expert is named by exactly 33 tokens and every other expert by 1 to 32 tokens. `slot_ids`: within a block of 128 tokens, the number of earlier tokens of the block with the same expert.
All inputs are finite; a program needn't handle non-finite values.
Results may differ from a plain program's by a relative error of at most 0.0062.
Values may be sent and summed in bfloat16 or wider, within the bound.
No kernel may reach another device: no remote copies, remote signals or barrier semaphores. Data moves between devices by JAX's collectives and lax.ppermute only.
A program may use at most 128 MiB of HBM per device.

v0:
```python
import jax
import jax.numpy as jnp
from jax import lax
from jax.sharding import PartitionSpec as P


def shifted(value, axis, steps):
    count = lax.axis_size(axis)
    leading, last = (max(0, -steps), min(count, count - steps))
    return lax.ppermute(value, axis, [(source, source + steps) for source in range(leading, last)])


def silu_parts(gate_value):
    sigm = jax.nn.sigmoid(gate_value)
    return (gate_value * sigm, sigm * (1.0 + gate_value * (1.0 - sigm)))


def routed_backward(slot_rows, slot_score, kept, gate_up, down):
    half = down.shape[0]
    gate_value = kept[:, :half].astype(jnp.float32)
    up_value = kept[:, half:].astype(jnp.float32)
    activated, slope = silu_parts(gate_value)
    hidden = (activated * up_value).astype(jnp.bfloat16)
    expert_out = jnp.dot(hidden, down, preferred_element_type=jnp.float32)
    inner_dot = jnp.sum(slot_rows.astype(jnp.float32) * expert_out, axis=1).astype(jnp.bfloat16)
    hidden_grad = slot_score.astype(jnp.float32)[:, None] * lax.dot_general(
        slot_rows, down, (((1,), (1,)), ((), ())), preferred_element_type=jnp.float32
    )
    hidden_grads = jnp.concatenate(
        [
            (hidden_grad * up_value * slope).astype(jnp.bfloat16),
            (hidden_grad * activated).astype(jnp.bfloat16),
        ],
        axis=1,
    )
    slot_dx = lax.dot_general(
        hidden_grads, gate_up, (((1,), (1,)), ((), ())), preferred_element_type=jnp.float32
    ).astype(jnp.bfloat16)
    return (slot_dx, inner_dot, hidden_grads)


def on_device(
    out_grad, expert_ids, slot_ids, router_logits, saved_routed, w_gate_up, w_down, w_router
):
    upstream = out_grad[0]
    routes = expert_ids[0]
    places = slot_ids[0]
    logits = router_logits[0]
    kept_routed = saved_routed[0, 0]
    pieces_total = lax.axis_size("expert")
    expert_count = logits.shape[1]
    group = pieces_total // expert_count
    capacity = kept_routed.shape[0]
    per_peer = capacity // pieces_total
    features = upstream.shape[1]
    target = routes * per_peer + places
    onehot = routes[:, None] == jnp.arange(expert_count, dtype=jnp.int32)[None, :]
    chosen = jnp.sum(jnp.where(onehot, logits, jnp.float32(0.0)), axis=1)
    gate_prob = jax.nn.sigmoid(chosen)
    gating = gate_prob.astype(jnp.bfloat16)
    local_rows = (
        jnp.zeros((expert_count * per_peer, features), jnp.bfloat16).at[target].set(upstream)
    )
    local_score = jnp.zeros((expert_count * per_peer,), jnp.bfloat16).at[target].set(gating)
    send_rows = jnp.broadcast_to(
        local_rows.reshape(expert_count, 1, per_peer, features),
        (expert_count, group, per_peer, features),
    ).reshape(pieces_total, per_peer, features)
    send_score = jnp.broadcast_to(
        local_score.reshape(expert_count, 1, per_peer), (expert_count, group, per_peer)
    ).reshape(pieces_total, per_peer)
    recv_rows, recv_score = (
        lax.all_to_all(send_rows, "expert", split_axis=0, concat_axis=0, tiled=True),
        lax.all_to_all(send_score, "expert", split_axis=0, concat_axis=0, tiled=True),
    )
    slot_dx, inner_dot, hidden_grads = routed_backward(
        recv_rows.reshape(capacity, features),
        recv_score.reshape(capacity),
        kept_routed,
        w_gate_up[0, 0],
        w_down[0, 0],
    )
    outgoing = (
        slot_dx.reshape(pieces_total, per_peer, features),
        inner_dot.reshape(pieces_total, per_peer),
    )
    rows_part = lax.all_to_all(outgoing[0], "expert", split_axis=0, concat_axis=0, tiled=True)
    inner_part = lax.all_to_all(outgoing[1], "expert", split_axis=0, concat_axis=0, tiled=True)
    count = rows_part.shape[1]
    rows_sum = jnp.sum(
        rows_part.astype(jnp.float32).reshape(expert_count, group, count, features), axis=1
    )
    inner_sum = jnp.sum(inner_part.astype(jnp.float32).reshape(expert_count, group, count), axis=1)
    flat_rows = rows_sum.reshape(expert_count * per_peer, features)
    flat_inner = inner_sum.reshape(expert_count * per_peer)
    returned = flat_rows[target]
    inner_tok = flat_inner[target]
    dlogit = gate_prob * (1.0 - gate_prob) * inner_tok
    coeffs = jnp.where(onehot, dlogit[:, None], jnp.float32(0.0))
    router_dx = jnp.dot(coeffs, w_router[0].astype(jnp.float32).T, precision=lax.Precision.HIGHEST)
    summed = (returned + router_dx).astype(jnp.bfloat16)
    previous = shifted(summed, "section", -1)
    return (previous[None], hidden_grads[None, None])


def solution(mesh):
    placed = (
        P("section", "expert", None),
        P("section", "expert"),
        P("section", "expert"),
        P("section", "expert", None),
        P("section", "expert", None, None),
        P("section", "expert", None, None),
        P("section", "expert", None, None),
        P("section", None, None),
    )
    return jax.shard_map(
        on_device,
        mesh=mesh,
        in_specs=placed,
        out_specs=(P("section", "expert", None), P("section", "expert", None, None)),
        check_vma=False,
    )
```

profile of v0, /device:TPU:0, one launch (start us, length us, event | category | flops | bytes accessed | tf_op | source)
XLA Modules:
  0.0 131.4 jit_solution(18341015863277831169)
XLA Ops:
  0.6 0.7 fusion.40
  1.4 0.4 copy-done
  1.8 1.7 %scatter_custom_fusion.1 = bf16[132,2560]{1,0:T(8,128)(2,1)S(1)} fusion(s32[128]{0:T(128)S(1)} %fusion.40, bf16[1,128,2560]{2,1,0:T(8,128)(2,1)S(1)} %copy-done, bf16[]{:T(256)} %constant.6.clone.1), kind=kCustom, calls=%fused_computation.34 | custom fusion | bytes 1331202 | tf_op jit(solution)/shard_map/scatter | solution.py:62
  3.4 0.2 broadcast_in_dim.52
  3.7 1.3 broadcast_in_dim.53
  4.9 5.3 %all-to-all-start.1 = ((bf16[8,33,2560]{2,1,0:T(8,128)(2,1)}), bf16[8,33,2560]{2,1,0:T(8,128)(2,1)S(1)}, u32[]{:S(2)}, u32[]{:S(2)}) async-start(bf16[8,33,2560]{2,1,0:T(8,128)(2,1)} %bitcast.44), calls=%async_computation.1 | async-start | bytes 3276800 | tf_op jit(solution)/shard_map/all_to_all | solution.py:73
  10.3 21.7 %all-to-all-done.1 = bf16[8,33,2560]{2,1,0:T(8,128)(2,1)S(1)} async-done(((bf16[8,33,2560]{2,1,0:T(8,128)(2,1)}), bf16[8,33,2560]{2,1,0:T(8,128)(2,1)S(1)}, u32[]{:S(2)}, u32[]{:S(2)}) %all-to-all-start.1) | async-done | bytes 1351712 | tf_op jit(solution)/shard_map/all_to_all | solution.py:73
  32.0 1.5 %reshape.106 = bf16[264,2560]{1,0:T(8,128)(2,1)} reshape(bf16[8,33,2560]{2,1,0:T(8,128)(2,1)S(1)} %all-to-all-done.1) | data formatting | bytes 2703360 | tf_op jit(solution)/shard_map/reshape | solution.py:77
  33.5 8.3 %fusion.24 = bf16[264]{0:T(512)(128)(2,1)S(1)} fusion(bf16[1,1,2048,2560]{3,2,1,0:T(8,128)(2,1)} %param.14, bf16[264,2560]{1,0:T(8,128)(2,1)} %reshape.106, bf16[264,4096]{1,0:T(8,128)(2,1)} %bitcast.50), kind=kOutput, calls=%fused_computation.31 | convolution fusion | flops 2774593280 | bytes 14000656 | tf_op jit(solution)/shard_map/dot_general | solution.py:24
  41.8 0.7 convert_element_type.81
  42.5 3.3 %all-to-all-start.3 = ((bf16[8,1,33]{2,1,0:T(2,128)(2,1)}), bf16[8,1,33]{2,1,0:T(2,128)(2,1)S(1)}, u32[]{:S(2)}, u32[]{:S(2)}) async-start(bf16[8,1,33]{2,1,0:T(2,128)(2,1)} %convert_element_type.81), calls=%async_computation.3 | async-start | bytes 8192 | tf_op jit(solution)/shard_map/all_to_all | solution.py:88
  45.8 4.5 %all-to-all-done.3 = bf16[8,1,33]{2,1,0:T(2,128)(2,1)S(1)} async-done(((bf16[8,1,33]{2,1,0:T(2,128)(2,1)}), bf16[8,1,33]{2,1,0:T(2,128)(2,1)S(1)}, u32[]{:S(2)}, u32[]{:S(2)}) %all-to-all-start.3) | async-done | bytes 560 | tf_op jit(solution)/shard_map/all_to_all | solution.py:88
  50.3 0.1 reshape.111
  50.4 1.3 gather_fusion.1
  51.7 1.3 %scatter_custom_fusion = bf16[132]{0:T(256)(128)(2,1)S(1)} fusion(s32[128]{0:T(128)S(1)} %fusion.40, bf16[128]{0:T(256)(128)(2,1)S(1)} %get-tuple-element.3, bf16[]{:T(256)} %constant.6.clone.1), kind=kCustom, calls=%fused_computation.52 | custom fusion | bytes 266 | tf_op jit(solution)/shard_map/scatter | solution.py:64
  53.0 0.1 broadcast_in_dim.49
  53.2 7.0 %all_to_all.25 = bf16[8,1,33]{2,1,0:T(2,128)(2,1)S(1)} all-to-all(bf16[8,1,33]{2,1,0:T(2,128)(2,1)S(1)} %copy.11), channel_id=1, replica_groups=mesh['section'=4,'expert'=8] {'expert'}, dimensions={0} | all-to-all | bytes 1056 | tf_op jit(solution)/shard_map/all_to_all | solution.py:74
  60.2 0.1 reshape.112
  60.3 8.1 %fusion.17 = (bf16[264,2048]{1,0:T(8,128)(2,1)S(1)}, bf16[264,2048]{1,0:T(8,128)(2,1)S(1)}) fusion(bf16[264,4096]{1,0:T(8,128)(2,1)} %bitcast.51, bf16[264,2560]{1,0:T(8,128)(2,1)S(1)} %copy-done.1, bf16[1,1,2048,2560]{3,2,1,0:T(8,128)(2,1)} %param.14, f32[264]{0:T(512)S(1)} %reshape.112), kind=kOutput, calls=%fused_computation.22 | convolution fusion | flops 2776891392 | bytes 16163872 | tf_op jit(solution)/shard_map/dot_general | solution.py:26
  68.4 1.0 copy-done.2
  69.4 0.3 copy-done.4
  69.7 11.7 %fusion.9 = bf16[264,2560]{1,0:T(8,128)(2,1)} fusion(bf16[1,1,2560,4096]{3,2,1,0:T(8,128)(2,1)} %param.13, bf16[264,2048]{1,0:T(8,128)(2,1)S(1)} %get-tuple-element.5, bf16[264,2048]{1,0:T(8,128)(2,1)S(1)} %get-tuple-element.4), kind=kOutput, calls=%fused_computation.11 | convolution fusion | flops 5541482496 | bytes 24485888 | tf_op jit(solution)/shard_map/dot_general | solution.py:36
  81.4 1.8 %reshape.107 = bf16[8,33,2560]{2,1,0:T(8,128)(2,1)S(1)} reshape(bf16[264,2560]{1,0:T(8,128)(2,1)} %fusion.9) | data formatting | bytes 2703360 | tf_op jit(solution)/shard_map/reshape | solution.py:84
  83.2 24.1 %all_to_all.26 = bf16[8,33,2560]{2,1,0:T(8,128)(2,1)S(1)} all-to-all(bf16[8,33,2560]{2,1,0:T(8,128)(2,1)S(1)} %reshape.107), channel_id=1, replica_groups=mesh['section'=4,'expert'=8] {'expert'}, dimensions={0} | all-to-all | bytes 2703360 | tf_op jit(solution)/shard_map/all_to_all | solution.py:87
  107.3 1.4 %convert_reduce_fusion = f32[4,33,2560]{2,1,0:T(8,128)} fusion(bf16[8,33,2560]{2,1,0:T(8,128)(2,1)S(1)} %all_to_all.26), kind=kLoop, calls=%fused_computation.14 | loop fusion | flops 1013760 | bytes 2703360 | tf_op jit(solution)/shard_map/reduce_sum | solution.py:90
  108.7 1.6 %reshape.110 = f32[132,2560]{1,0:T(8,128)S(1)} reshape(f32[4,33,2560]{2,1,0:T(8,128)} %convert_reduce_fusion) | data formatting | bytes 2703360 | tf_op jit(solution)/shard_map/reshape | solution.py:94
  110.4 1.1 gather_fusion
  111.5 0.7 fusion.12
  112.3 1.3 collective-permute-start
  113.6 2.8 %fusion.27 = bf16[1,1,264,4096]{3,2,1,0:T(8,128)(2,1)} fusion(bf16[264,2048]{1,0:T(8,128)(2,1)} %copy-done.4, bf16[264,2048]{1,0:T(8,128)(2,1)S(1)} %copy-done.3), kind=kLoop, calls=%fused_computation.32 | loop fusion | flops 4325376 | bytes 4325376 | tf_op jit(solution)/shard_map/broadcast_in_dim | solution.py:103
  116.4 14.2 %collective-permute-done = bf16[128,2560]{1,0:T(8,128)(2,1)S(1)} collective-permute-done((bf16[128,2560]{1,0:T(8,128)(2,1)S(1)}, bf16[128,2560]{1,0:T(8,128)(2,1)S(1)}, u32[]{:S(2)}, u32[]{:S(2)}) %collective-permute-start) | collective-permute-done | bytes 655392 | tf_op jit(solution)/shard_map/ppermute | solution.py:10
  130.6 0.8 copy.14
  (21 shorter events, 0.1 us)
Async XLA Ops:
  0.6 1.1 copy-start
  4.9 5.3 %copy-start.6 = (s32[1,128]{1,0:T(1,128)S(1)}, s32[1,128]{1,0:T(1,128)}, u32[]{:S(2)}) copy-start(s32[1,128]{1,0:T(1,128)} %param.9) | copy-start | bytes 1540
  4.9 5.3 %copy-start.7 = (f32[1,128,4]{1,2,0:T(4,128)S(1)}, f32[1,128,4]{1,2,0:T(4,128)}, u32[]{:S(2)}) copy-start(f32[1,128,4]{1,2,0:T(4,128)} %param.11) | copy-start | bytes 6148
  4.9 27.0 %all-to-all-start.1 = ((bf16[8,33,2560]{2,1,0:T(8,128)(2,1)}), bf16[8,33,2560]{2,1,0:T(8,128)(2,1)S(1)}, u32[]{:S(2)}, u32[]{:S(2)}) async-start(bf16[8,33,2560]{2,1,0:T(8,128)(2,1)} %bitcast.44), calls=%async_computation.1 | async-start | bytes 3276800 | tf_op jit(solution)/shard_map/all_to_all | solution.py:73
  33.5 26.8 %copy-start.1 = (bf16[264,2560]{1,0:T(8,128)(2,1)S(1)}, bf16[264,2560]{1,0:T(8,128)(2,1)}, u32[]{:S(2)}) copy-start(bf16[264,2560]{1,0:T(8,128)(2,1)} %reshape.106) | copy-start | bytes 4055044
  42.5 7.8 %all-to-all-start.3 = ((bf16[8,1,33]{2,1,0:T(2,128)(2,1)}), bf16[8,1,33]{2,1,0:T(2,128)(2,1)S(1)}, u32[]{:S(2)}, u32[]{:S(2)}) async-start(bf16[8,1,33]{2,1,0:T(2,128)(2,1)} %convert_element_type.81), calls=%async_computation.3 | async-start | bytes 8192 | tf_op jit(solution)/shard_map/all_to_all | solution.py:88
  68.4 1.0 copy-start.2
  68.4 1.3 %copy-start.4 = (bf16[264,2048]{1,0:T(8,128)(2,1)}, bf16[264,2048]{1,0:T(8,128)(2,1)S(1)}, u32[]{:S(2)}) copy-start(bf16[264,2048]{1,0:T(8,128)(2,1)S(1)} %get-tuple-element.5) | copy-start | bytes 3244036
  110.4 1.1 copy-start.5
  111.5 2.1 %copy-start.3 = (bf16[264,2048]{1,0:T(8,128)(2,1)S(1)}, bf16[264,2048]{1,0:T(8,128)(2,1)}, u32[]{:S(2)}) copy-start(bf16[264,2048]{1,0:T(8,128)(2,1)} %copy-done.2) | copy-start | bytes 3244036
  112.3 18.3 %collective-permute-start = (bf16[128,2560]{1,0:T(8,128)(2,1)S(1)}, bf16[128,2560]{1,0:T(8,128)(2,1)S(1)}, u32[]{:S(2)}, u32[]{:S(2)}) collective-permute-start(bf16[128,2560]{1,0:T(8,128)(2,1)S(1)} %fusion.12), channel_id=1, source_target_pairs={{8,0},{16,8},{24,16},{9,1},{17,9},{25,17},{10,2},{18,10},{26,18},{... | collective-permute-start | bytes 1966088 | tf_op jit(solution)/shard_map/ppermute | solution.py:10
where the time goes:
time: 132 us; the launch traced here: 131 us
  waiting for transfers between devices  40.4 us (31%)
  blocking collectives  31.1 us (24%)
  matrix products  28.8 us (22%)
  local copies, waits for them, and re-layouts  15.3 us (12%)
  starting transfers between devices  9.9 us (8%)
  other arithmetic  5.08 us (4%)
    all_to_all x1, blocking collectives, on_device(): lax.all_to_all(outgoing[0], 'expert', split_axis=0, concat_axis=0, tiled=...  24.1 us
    all_to_all x1, waiting for transfers between devices, on_device(): lax.all_to_all(send_rows, 'expert', split_axis=0, concat_axis=0, tiled=True)  21.7 us
    ppermute x1, waiting for transfers between devices, shifted(): lax.ppermute(value, axis, [(source, source + steps) for source in range(l...  14.2 us
    dot_general x1, matrix products, routed_backward(): lax.dot_general(hidden_grads, gate_up, (((1,), (1,)), ((), ())), preferre...  11.7 us
    dot_general x1, matrix products, routed_backward(): expert_out = jnp.dot(hidden, down, preferred_element_type=jnp.float32)  8.27 us
    dot_general x1, matrix products, routed_backward(): lax.dot_general(slot_rows, down, (((1,), (1,)), ((), ())), preferred_elem...  8.08 us
    all_to_all x1, blocking collectives, on_device(): lax.all_to_all(send_score, 'expert', split_axis=0, concat_axis=0, tiled=T...  7.02 us
    all_to_all x1, starting transfers between devices, on_device(): lax.all_to_all(send_rows, 'expert', split_axis=0, concat_axis=0, tiled=True)  5.3 us
  transfers between devices with their start and end apart: 3, of which 3 were waited for; matrix products, arithmetic and copies ran while one was open for 2% of the time, Pallas kernels for 0%

commit v1 on v0

v1 whole, which is shorter than its diff:
```python
import functools
import math

import jax
import jax.numpy as jnp
from jax import lax
from jax.experimental import pallas as pl
from jax.experimental.pallas import tpu as pltpu
from jax.sharding import PartitionSpec as P

LANES = 128
VMEM = pl.BlockSpec(memory_space=pltpu.VMEM)
SMEM = pl.BlockSpec(memory_space=pltpu.SMEM)
HBM = pl.BlockSpec(memory_space=pltpu.HBM)
F32 = jnp.float32
BF16 = jnp.bfloat16


SCORE, SLOPE_HIGH, SLOPE_LOW, TOKEN, LAST_TOKEN = range(5)


def iota(shape, axis):
    return lax.broadcasted_iota(jnp.int32, shape, axis)


def nt_dot(a, b):
    return lax.dot_general(a, b, (((1,), (1,)), ((), ())), preferred_element_type=F32)


def one_hot(mask):
    return mask.astype(F32).astype(BF16)


def dot(a, b):
    return jnp.dot(a, b, preferred_element_type=F32)


def pack_kernel(experts, main, me, up_in, route_in, slot_in, logit_in, *refs):
    outs, refs = refs[:experts], refs[experts:]
    up_ref, route_ref, slot_ref, logit_ref, sems = refs
    copies = [
        pltpu.make_async_copy(source, target, sems.at[i])
        for i, (source, target) in enumerate(
            ((route_in, route_ref), (slot_in, slot_ref), (logit_in, logit_ref), (up_in, up_ref))
        )
    ]
    for copy in copies:
        copy.start()
    for copy in copies[:-1]:
        copy.wait()
    tokens, width = up_ref.shape
    parts = width // LANES
    route, slot = route_ref[...], slot_ref[...]
    chosen = jnp.zeros((1, tokens), F32)
    for e in range(experts):
        chosen += jnp.where(route == e, logit_ref[e : e + 1, :], 0.0)
    gate = jax.nn.sigmoid(chosen)
    slope = gate * (1.0 - gate)
    high = slope.astype(BF16).astype(F32)
    number = (iota((1, tokens), 1) + 1).astype(F32)
    turn = lax.rem(route - me[0] + experts, experts)
    place = turn * main + slot
    rows = iota((experts * main, tokens), 0)
    pick = ((rows == place) & (slot < main)).astype(F32).astype(BF16)
    top = iota((8, tokens), 0)
    last = ((top == turn) & (slot == main)).astype(F32)
    mine = (top == turn).astype(F32)
    values = jnp.concatenate(
        [mine * v for v in (gate.astype(BF16).astype(F32), high, slope - high)], axis=0
    )
    stats = nt_dot(values.astype(BF16), one_hot(iota((LANES, tokens), 0) == slot))
    by_place = one_hot((iota((LANES, tokens), 0) == place) & (slot < main))
    token = nt_dot((mine * number).astype(BF16), by_place)
    by_turn = one_hot((iota((LANES, tokens), 0) == turn) & (slot == main))
    last_token = nt_dot((mine * number).astype(BF16), by_turn)
    copies[-1].wait()
    upstream = up_ref[...]
    packed = dot(pick, upstream)
    last_rows = dot(last.astype(BF16), upstream)
    side_row = iota((main, LANES), 0)
    for k in range(experts):
        outs[k][:, :width] = packed[k * main : (k + 1) * main].astype(BF16)
        side = jnp.zeros((main, LANES), F32)
        for c in range(parts):
            side = jnp.where(side_row == c, last_rows[k : k + 1, c * LANES : (c + 1) * LANES], side)
        for c, row in (
            (SCORE, stats[k : k + 1]),
            (SLOPE_HIGH, stats[8 + k : 9 + k]),
            (SLOPE_LOW, stats[16 + k : 17 + k]),
            (TOKEN, token[k : k + 1]),
            (LAST_TOKEN, last_token[k : k + 1]),
        ):
            side = jnp.where(side_row == parts + c, row, side)
        outs[k][:, width:] = side.astype(BF16)


def arrival_row(natural, me, experts, group, main, total):
    per = main + 1
    source, slot = natural // per, lax.rem(natural, per)
    turn = lax.rem(me[0] - source // group + experts, experts)
    lane = lax.rem(lax.rem(source, group) - me[1] + group, group)
    block = lane * experts + turn
    return jnp.where(slot < main, block * main + slot, total * main + block)


def copies_of(source, first, targets, sems):
    step = targets[0].shape[0]
    return [
        pltpu.make_async_copy(source.at[(first + i) * step : (first + i + 1) * step], target, sems.at[i])
        for i, target in enumerate(targets)
    ]


def window_kernel(experts, group, main, chunks, me, kept_in, down_in, weight_in, out_ref, *refs):
    downs, weights, refs = refs[: chunks[0]], refs[chunks[0] : -4], refs[-4:]
    kept_ref, kept_sem, down_sems, weight_sems = refs
    kept_copy = pltpu.make_async_copy(kept_in, kept_ref, kept_sem)
    kept_copy.start()
    copies = copies_of(down_in, 0, downs, down_sems) + copies_of(weight_in, 0, weights, weight_sems)
    for copy in copies:
        copy.start()
    rows, columns = out_ref.shape
    place = arrival_row(iota((1, rows), 1), me, experts, group, main, experts * group)
    pick = one_hot(iota((rows, rows), 0) == place)
    kept_copy.wait()
    step = min(1024, columns)
    for c in range(0, columns, step):
        out_ref[:, c : c + step] = dot(pick, kept_ref[:, c : c + step]).astype(BF16)
    for copy in copies:
        copy.wait()


def restore_kernel(experts, group, main, me, grad_ref, out_ref):
    rows = grad_ref.shape[0]
    place = arrival_row(iota((rows, 1), 0), me, experts, group, main, experts * group)
    out_ref[...] = dot(one_hot(iota((rows, rows), 1) == place), grad_ref[...]).astype(BF16)


def silu_parts(gate_value):
    sigm = jax.nn.sigmoid(gate_value)
    return (gate_value * sigm, sigm * (1.0 + gate_value * (1.0 - sigm)))


def expert_kernel(experts, group, main, chunks, fetched, me, *refs):
    total = experts * group
    blocks, refs = refs[:total], refs[total:]
    downs, refs = refs[: chunks[0]], refs[chunks[0] :]
    weights, refs = refs[:fetched], refs[fetched:]
    kept_ref, router_ref, weight_in, grad_ref, own_ref, last_ref = refs[:6]
    sends, refs = refs[6 : 5 + group], refs[5 + group :]
    late, (rows, raw_a, raw_b, late_sems) = refs[:-4], refs[-4:]
    late_copies = copies_of(weight_in, fetched, late, late_sems)
    for copy in late_copies:
        copy.start()
    raws = (raw_a, raw_b)
    count, width = rows.shape
    parts = width // LANES
    half = kept_ref.shape[1] // 2
    full, own = total * main, experts * main

    sides = []
    for n in range(total):
        rows[n * main : (n + 1) * main, :] = blocks[n][:, :width]
        sides.append(blocks[n][:, width:])
    sides = jnp.concatenate(sides, axis=0)
    wanted = iota((parts * total, full), 0)
    pick = iota((parts * total, full), 1) == lax.rem(wanted, total) * main + wanted // total
    last = dot(one_hot(pick), sides)
    for c in range(parts):
        rows[full:, c * LANES : (c + 1) * LANES] = last[c * total : (c + 1) * total].astype(BF16)
    row = iota((count, 1), 0)
    block = jnp.where(row < full, row // main, row - full)
    slot = jnp.where(row < full, lax.rem(row, main), main)
    own_lane = iota((count, LANES), 1) == slot

    def column(which):
        choose = iota((count, full), 1) == block * main + parts + which
        return jnp.sum(jnp.where(own_lane, dot(one_hot(choose), sides), 0.0), axis=1, keepdims=True)

    score = column(SCORE)
    slope = column(SLOPE_HIGH) + column(SLOPE_LOW)
    step = raw_a.shape[1]
    inner = jnp.zeros((count, LANES), F32)

    def finish(start, raw, inner):
        piece, other = slice(start, start + step), slice(half + start, half + start + step)
        up_value = kept_ref[:, other].astype(F32)
        activated, bend = silu_parts(kept_ref[:, piece].astype(F32))
        hidden = (activated * up_value).astype(BF16).astype(F32)
        hidden_grad = score * raw
        grad_ref[:, piece] = (hidden_grad * up_value * bend).astype(BF16)
        grad_ref[:, other] = (hidden_grad * activated).astype(BF16)
        product = hidden * raw
        return inner + sum(product[:, c : c + LANES] for c in range(0, step, LANES))

    for i in range(half // step):
        raws[i % 2][...] = nt_dot(rows[...], downs[i][...])
        if i:
            inner = finish((i - 1) * step, raws[(i - 1) % 2][...], inner)
    inner = finish(half - step, raws[(half // step - 1) % 2][...], inner)
    coeff = slope * jnp.sum(inner, axis=1, keepdims=True)

    step = late[0].shape[0]
    for i, weight_ref in enumerate(list(weights) + list(late)):
        if i >= fetched:
            late_copies[i - fetched].wait()
        piece = slice(i * step, (i + 1) * step)
        router = router_ref[:, piece].astype(F32)
        router = sum(jnp.where(me[0] == e, router[e : e + 1], 0.0) for e in range(experts))
        partial = nt_dot(grad_ref[...], weight_ref[...]) + coeff * router
        last = partial[full:]
        own_ref[:, piece] = partial[:own]
        last_ref[:, piece] = last
        for lane in range(1, group):
            out = sends[lane - 1]
            out[:own, piece] = partial[lane * own : (lane + 1) * own].astype(BF16)
            out[own : own + total, piece] = last.astype(BF16)
            if out.shape[0] > own + total:
                out[own + total :, piece] = jnp.zeros((out.shape[0] - own - total, step), BF16)


def merge_kernel(experts, group, main, own_ref, last_ref, *refs):
    others = refs[: group - 1]
    sides = refs[group - 1 : group - 1 + experts]
    outs = refs[group - 1 + experts :]
    width = own_ref.shape[1]
    parts = width // LANES
    own = experts * main
    total = experts * group
    lasts = [other[own : own + total, :].astype(F32) for other in others]
    side_row = iota((main, LANES), 0)
    for k in range(experts):
        value = own_ref[k * main : (k + 1) * main, :]
        last = last_ref[k : k + 1, :]
        for lane, other in enumerate(others, 1):
            value += other[k * main : (k + 1) * main, :].astype(F32)
            row = lane * experts + k
            last += lasts[lane - 1][row : row + 1, :]
        outs[k][:, :width] = value.astype(BF16)
        side = sides[k][:, width:].astype(F32)
        for c in range(parts):
            side = jnp.where(side_row == c, last[:, c * LANES : (c + 1) * LANES], side)
        outs[k][:, width:] = side.astype(BF16)


def tokens_kernel(experts, main, *refs):
    blocks, (out_ref, rows) = refs[:experts], refs[experts:]
    tokens, width = out_ref.shape
    parts = width // LANES
    sides = []
    for k in range(experts):
        rows[k * main : (k + 1) * main, :] = blocks[k][:, :width]
        sides.append(blocks[k][:, width:])
    token = sum(side[parts + TOKEN : parts + TOKEN + 1].astype(F32) for side in sides)
    last_token = sum(side[parts + LAST_TOKEN : parts + LAST_TOKEN + 1].astype(F32) for side in sides)
    sides = jnp.concatenate(sides, axis=0)
    height = rows.shape[0] - experts * main
    wanted = iota((parts * height, experts * main), 0)
    turn = lax.rem(wanted, height)
    pick = (iota((parts * height, experts * main), 1) == turn * main + wanted // height) & (turn < experts)
    last = dot(pick.astype(F32).astype(BF16), sides)
    for c in range(parts):
        rows[experts * main :, c * LANES : (c + 1) * LANES] = last[c * height : (c + 1) * height].astype(
            BF16
        )
    number = (iota((tokens, LANES), 0) + 1).astype(F32)
    main_pick = (number == token).astype(F32).astype(BF16)
    last_pick = (number == last_token).astype(F32).astype(BF16)
    pick = jnp.concatenate([main_pick[:, : experts * main], last_pick[:, :height]], axis=1)
    out_ref[...] = dot(pick, rows[...]).astype(BF16)


def call(kernel, outs, ins, flops=0, limit=4, **options):
    ins = [
        pltpu.with_memory_space_constraint(x, pltpu.HBM) if spec is HBM else x
        for x, spec in zip(ins, options["in_specs"])
    ]
    moved = sum(math.prod(x.shape) * jnp.dtype(x.dtype).itemsize for x in list(ins) + list(outs))
    return pl.pallas_call(
        kernel,
        out_shape=tuple(outs),
        cost_estimate=pl.CostEstimate(flops=int(flops), bytes_accessed=int(moved), transcendentals=0),
        compiler_params=pltpu.CompilerParams(vmem_limit_bytes=limit * 1024 * 1024),
        **options,
    )(*ins)


def grant(scratch, more):
    return more + -(-sum(math.prod(x.shape) * jnp.dtype(x.dtype).itemsize for x in scratch) // 2**20)


def on_device(
    out_grad, expert_ids, slot_ids, router_logits, saved_routed, w_gate_up, w_down, w_router
):
    sections, total = lax.axis_size("section"), lax.axis_size("expert")
    tokens, width = out_grad.shape[1:]
    experts = router_logits.shape[2]
    group = total // experts
    capacity = saved_routed.shape[2]
    half = w_down.shape[2]
    main = capacity // total - 1
    own = experts * main
    assert own <= LANES and tokens <= 255 and width // LANES + 5 <= main and experts <= 8
    position = lax.axis_index("expert")
    me = jnp.stack([position // group, position % group]).astype(jnp.int32)
    block = jax.ShapeDtypeStruct((main, width + LANES), BF16)

    def shape(*dims, dtype=BF16):
        return jax.ShapeDtypeStruct(dims, dtype)

    def send(value, turn, lane):
        pairs = []
        for source in range(total):
            e, g = source // group, source % group
            pairs.append((source, (e + turn) % experts * group + (g - lane) % group))
        return lax.ppermute(value, "expert", pairs)

    def send_back(value, turn):
        pairs = []
        for section in range(1, sections):
            for source in range(total):
                e, g = source // group, source % group
                target = (e - turn) % experts * group + g
                pairs.append((section * total + source, (section - 1) * total + target))
        return lax.ppermute(value, ("section", "expert"), pairs)

    packed = call(
        functools.partial(pack_kernel, experts, main),
        [block] * experts,
        [me, out_grad[0], expert_ids, slot_ids, router_logits[0].T],
        2 * own * tokens * width,
        in_specs=[SMEM] + [HBM] * 4,
        out_specs=[VMEM] * experts,
        scratch_shapes=[
            pltpu.VMEM((tokens, width), BF16),
            pltpu.VMEM((1, tokens), jnp.int32),
            pltpu.VMEM((1, tokens), jnp.int32),
            pltpu.VMEM((experts, tokens), F32),
            pltpu.SemaphoreType.DMA((4,)),
        ],
    )
    held = [packed[0]] + [send(packed[k], k, 0) for k in range(1, experts)]
    first = [send(packed[0], 0, lane) for lane in range(1, group)]

    chunks = (max(1, half // 512), max(1, width // 512))
    fetched = chunks[1] - 2
    down_shape, weight_shape = (half // chunks[0], width), (width // chunks[1], 2 * half)
    ordered, *weights = call(
        functools.partial(window_kernel, experts, group, main, chunks),
        [shape(capacity, 2 * half)]
        + [pltpu.VMEM(down_shape, BF16)] * chunks[0]
        + [pltpu.VMEM(weight_shape, BF16)] * fetched,
        [me, saved_routed[0, 0], w_down[0, 0], w_gate_up[0, 0]],
        2 * capacity * capacity * 2 * half,
        8,
        in_specs=[SMEM] + [HBM] * 3,
        out_specs=[VMEM] * (1 + chunks[0] + fetched),
        scratch_shapes=[
            pltpu.VMEM((capacity, 2 * half), BF16),
            pltpu.SemaphoreType.DMA,
            pltpu.SemaphoreType.DMA((chunks[0],)),
            pltpu.SemaphoreType.DMA((fetched,)),
        ],
    )
    held[1:], ordered = lax.optimization_barrier((held[1:], ordered))
    arrived = list(held)
    rest = jnp.concatenate(held[1:], axis=0)
    for lane in range(1, group):
        other = send(rest, 0, lane)
        arrived.append(first[lane - 1])
        arrived += [other[k * main : (k + 1) * main] for k in range(experts - 1)]

    padded = own + -(-total // 16) * 16
    scratch = [pltpu.VMEM(weight_shape, BF16)] * (chunks[1] - fetched) + [
        pltpu.VMEM((capacity, width), BF16),
        pltpu.VMEM((capacity, down_shape[0]), F32),
        pltpu.VMEM((capacity, down_shape[0]), F32),
    ]
    grads, own_part, last_part, *sent = call(
        functools.partial(expert_kernel, experts, group, main, chunks, fetched),
        [
            shape(capacity, 2 * half),
            shape(own, width, dtype=F32),
            shape(total, width, dtype=F32),
        ]
        + [shape(padded, width)] * (group - 1),
        [me, *arrived]
        + [pltpu.with_memory_space_constraint(x, pltpu.VMEM) for x in weights]
        + [ordered, w_router[0].T, w_gate_up[0, 0]],
        6 * capacity * width * half,
        grant(scratch, 6),
        in_specs=[SMEM] + [VMEM] * (total + 2 + chunks[0] + fetched) + [HBM],
        out_specs=[VMEM] * (2 + group),
        scratch_shapes=scratch + [pltpu.SemaphoreType.DMA((chunks[1] - fetched,))],
    )
    others = [send(sent[lane - 1], 0, -lane) for lane in range(1, group)]

    merged = call(
        functools.partial(merge_kernel, experts, group, main),
        [block] * experts,
        [own_part, last_part] + others + held,
        own * width * group,
        in_specs=[VMEM] * (1 + group + experts),
        out_specs=[VMEM] * experts,
    )
    returned = [send_back(merged[k], k) for k in range(experts)]

    columns = min(1024, 2 * half)
    (hidden_grads,) = call(
        functools.partial(restore_kernel, experts, group, main),
        [shape(capacity, 2 * half)],
        [me, grads],
        2 * capacity * capacity * 2 * half,
        12,
        grid=(2 * half // columns,),
        in_specs=[SMEM, pl.BlockSpec((capacity, columns), lambda i: (0, i))],
        out_specs=[pl.BlockSpec((capacity, columns), lambda i: (0, i))],
    )
    (previous,) = call(
        functools.partial(tokens_kernel, experts, main),
        [shape(tokens, width)],
        returned,
        2 * own * tokens * width,
        in_specs=[VMEM] * experts,
        out_specs=[VMEM],
        scratch_shapes=[pltpu.VMEM((own + 16, width), BF16)],
    )
    return (previous[None], hidden_grads[None, None])


def solution(mesh):
    placed = (
        P("section", "expert", None),
        P("section", "expert"),
        P("section", "expert"),
        P("section", "expert", None),
        P("section", "expert", None, None),
        P("section", "expert", None, None),
        P("section", "expert", None, None),
        P("section", None, None),
    )
    return jax.shard_map(
        on_device,
        mesh=mesh,
        in_specs=placed,
        out_specs=(P("section", "expert", None), P("section", "expert", None, None)),
        check_vma=False,
    )
```

time: 132 us -> 54.6 us (0.41)
  blocking collectives: 31.1 us -> 0 us
  matrix products: 28.8 us -> 0 us
  Pallas kernels: 0 us -> 27.2 us
  waiting for transfers between devices: 40.4 us -> 14.4 us
  local copies, waits for them, and re-layouts: 15.3 us -> 0.04 us
  other arithmetic: 5.08 us -> 0.11 us
  starting transfers between devices: 9.9 us -> 11.9 us
    all_to_all x2 -> x0, blocking collectives: 31.1 us -> none  [the longest x1 24.1 us: on_device(): lax.all_to_all(outgoing[0], 'expert', split_axis=0, concat_axis=0, tiled=...]
    dot_general x4 -> x0, matrix products: 28.8 us -> none  [the longest x1 11.7 us: routed_backward(): lax.dot_general(hidden_grads, gate_up, (((1,), (1,)), ((), ())), preferre...]
    pallas_call x0 -> x6, Pallas kernels: none -> 27.2 us  [call(): pl.pallas_call(kernel, out_shape=tuple(outs), cost_estimate=pl.CostEstima...]
    all_to_all x2 -> x0, waiting for transfers between devices: 26.2 us -> none  [the longest x1 21.7 us: on_device(): lax.all_to_all(send_rows, 'expert', split_axis=0, concat_axis=0, tiled=True)]
    ppermute x1 -> x10, starting transfers between devices: 1.29 us -> 11.9 us  [the longest x6 6.71 us: send(): return lax.ppermute(value, 'expert', pairs)]
    all_to_all x2 -> x0, starting transfers between devices: 8.61 us -> none  [the longest x1 5.3 us: on_device(): lax.all_to_all(send_rows, 'expert', split_axis=0, concat_axis=0, tiled=True)]
    reshape x4 -> x0, local copies, waits for them, and re-layouts: 5.01 us -> none  [the longest x1 1.77 us: on_device(): slot_dx.reshape(pieces_total, per_peer, features)]
    scatter x2 -> x0, local copies, waits for them, and re-layouts: 3.03 us -> none  [the longest x1 1.68 us: on_device(): jnp.zeros((expert_count * per_peer, features), jnp.bfloat16).at[target]]
  transfers between devices with their start and end apart: 3 -> 10, of which waited for: 3 -> 6; matrix products, arithmetic and copies ran while one was open for 2% -> 0% of each run, Pallas kernels for 0% -> 24%
where the time goes in v1:
time: 54.6 us; the launch traced here: 54.3 us
  Pallas kernels  27.2 us (50%)
  waiting for transfers between devices  14.4 us (26%)
  starting transfers between devices  11.9 us (22%)
  between operations  0.76 us (1%)
    pallas_call x6, Pallas kernels, call(): pl.pallas_call(kernel, out_shape=tuple(outs), cost_estimate=pl.CostEstima...  27.2 us
    ppermute x4, waiting for transfers between devices, send_back(): return lax.ppermute(value, ('section', 'expert'), pairs)  10.7 us
    ppermute x6, starting transfers between devices, send(): return lax.ppermute(value, 'expert', pairs)  6.71 us
    ppermute x4, starting transfers between devices, send_back(): return lax.ppermute(value, ('section', 'expert'), pairs)  5.17 us
    ppermute x6, waiting for transfers between devices, send(): return lax.ppermute(value, 'expert', pairs)  3.68 us
  transfers between devices with their start and end apart: 10, of which 6 were waited for; matrix products, arithmetic and copies ran while one was open for 0% of the time, Pallas kernels for 24%

profile of v1, /device:TPU:0, one launch (start us, length us, event | category | flops | bytes accessed | tf_op | source)
XLA Modules:
  0.0 54.3 jit_solution(18138855340885699317)
XLA Ops:
  0.6 0.1 pad_add_fusion.me
  0.7 2.1 %shard_map.95 = (bf16[32,2688]{1,0:T(8,128)(2,1)S(1)}, bf16[32,2688]{1,0:T(8,128)(2,1)S(1)}, bf16[32,2688]{1,0:T(8,128)(2,1)S(1)}, bf16[32,2688]{1,0:T(8,128)(2,1)S(1)}) custom-call(s32[2]{0:T(128)S(1)} %pad_add_fusion.me, bf16[128,2560]{1,0:T(8,128)(2,1)} %bitcast.20, s32[1,128]{1,0:T(1,128)} %route_in.1, s32[1,128]{1,0:T(1,128)} %slot_in.1, f32[4,128]{1,0:T(4,128)} %bitcast.22), custom_call_target="tpu_custom_call" | custom-call | flops 83886080 | bytes 1346568 | tf_op jit(solution)/shard_map/pallas_call | solution.py:279
  2.9 3.0 %collective-permute-start = (bf16[32,2688]{1,0:T(8,128)(2,1)S(1)}, bf16[32,2688]{1,0:T(8,128)(2,1)S(1)}, u32[]{:S(2)}, u32[]{:S(2)}) collective-permute-start(bf16[32,2688]{1,0:T(8,128)(2,1)S(1)} %get-tuple-element.27), channel_id=1, source_target_pairs={{0,2},{1,3},{2,4},{3,5},{4,6},{5,7},{6,0},{7,1},{8,10},{9,11},{10,... | collective-permute-start | bytes 516104 | tf_op jit(solution)/shard_map/ppermute | solution.py:316
  5.8 1.5 %collective-permute-start.1 = (bf16[32,2688]{1,0:T(8,128)(2,1)S(1)}, bf16[32,2688]{1,0:T(8,128)(2,1)S(1)}, u32[]{:S(2)}, u32[]{:S(2)}) collective-permute-start(bf16[32,2688]{1,0:T(8,128)(2,1)S(1)} %get-tuple-element.28), channel_id=1, source_target_pairs={{0,4},{1,5},{2,6},{3,7},{4,0},{5,1},{6,2},{7,3},{8,12},{9,13},{10,... | collective-permute-start | bytes 516104 | tf_op jit(solution)/shard_map/ppermute | solution.py:316
  7.4 1.4 %collective-permute-start.2 = (bf16[32,2688]{1,0:T(8,128)(2,1)S(1)}, bf16[32,2688]{1,0:T(8,128)(2,1)S(1)}, u32[]{:S(2)}, u32[]{:S(2)}) collective-permute-start(bf16[32,2688]{1,0:T(8,128)(2,1)S(1)} %get-tuple-element.29), channel_id=1, source_target_pairs={{0,6},{1,7},{2,0},{3,1},{4,2},{5,3},{6,4},{7,5},{8,14},{9,15},{10,... | collective-permute-start | bytes 516104 | tf_op jit(solution)/shard_map/ppermute | solution.py:316
  8.8 0.0 copy-start
  8.8 8.9 %shard_map.96 = (bf16[264,4096]{1,0:T(8,128)(2,1)S(1)}, bf16[512,2560]{1,0:T(8,128)(2,1)S(1)}, bf16[512,2560]{1,0:T(8,128)(2,1)S(1)}, bf16[512,2560]{1,0:T(8,128...) custom-call(s32[2]{0:T(128)S(1)} %pad_add_fusion.me, ...), custom_call_target="tpu_custom_call" | custom-call | flops 570949632 | bytes 58851336 | tf_op jit(solution)/shard_map/pallas_call | solution.py:279
  17.7 0.0 collective-permute-done.refs_1_.refs_2_
  17.7 0.0 collective-permute-done.1.refs_2_.refs_3_
  17.7 0.0 collective-permute-done.2.refs_3_.refs_4_
  17.8 0.1 collective-permute-start.4
  17.9 0.5 collective-permute-start.3
  18.4 1.4 %collective-permute-done.4 = bf16[96,2688]{1,0:T(8,128)(2,1)S(1)} collective-permute-done((bf16[96,2688]{1,0:T(8,128)(2,1)S(1)}, bf16[96,2688]{1,0:T(8,128)(2,1)S(1)}, u32[]{:S(2)}, u32[]{:S(2)}) %collective-permute-start.4) | collective-permute-done | bytes 516128 | tf_op jit(solution)/shard_map/ppermute | solution.py:316
  19.8 0.2 collective-permute-done.3.refs_4_
  20.0 0.0 copy-done
  20.0 10.6 %shard_map.97 = (bf16[264,4096]{1,0:T(8,128)(2,1)S(1)}, f32[128,2560]{1,0:T(8,128)S(1)}, f32[8,2560]{1,0:T(8,128)S(1)}, bf16[144,2560]{1,0:T(8,128)(2,1)S(1)}) custom-call(s32[2]{0:T(128)S(1)} %pad_add_fusion.me, bf16[32,2688]{1,0:T(8,128)(2,1)S(1)} %get-tuple-element.26.refs_0_.refs_1_, bf16[32,2688]{1,0:T(8,128)(2,1)S(1)} %collective-permute-done.refs_1_.refs_2_, ...), custom_call_target="tpu_custom_call" | custom-call | flops 8304721920 | bytes 51892232 | tf_op jit(solution)/shard_map/pallas_call | solution.py:279
  30.6 0.2 collective-permute-start.5
  30.8 2.1 %collective-permute-done.5.refs_0_ = bf16[144,2560]{1,0:T(8,128)(2,1)S(1)} collective-permute-done((bf16[144,2560]{1,0:T(8,128)(2,1)S(1)}, bf16[144,2560]{1,0:T(8,128)(2,1)S(1)}, u32[]{:S(2)}, u32[]{:S(2)}) %collective-permute-start.5) | collective-permute-done | bytes 737312 | tf_op jit(solution)/shard_map/ppermute | solution.py:316
  32.9 0.2 shard_map.98
  33.0 1.3 %collective-permute-start.6 = (bf16[32,2688]{1,0:T(8,128)(2,1)S(1)}, bf16[32,2688]{1,0:T(8,128)(2,1)S(1)}, u32[]{:S(2)}, u32[]{:S(2)}) collective-permute-start(bf16[32,2688]{1,0:T(8,128)(2,1)S(1)} %get-tuple-element.45), channel_id=1, source_target_pairs={{8,0},{9,1},{10,2},{11,3},{12,4},{13,5},{14,6},{15,7},{16,8},{17,9... | collective-permute-start | bytes 516104 | tf_op jit(solution)/shard_map/ppermute | solution.py:325
  34.3 1.3 %collective-permute-start.7 = (bf16[32,2688]{1,0:T(8,128)(2,1)S(1)}, bf16[32,2688]{1,0:T(8,128)(2,1)S(1)}, u32[]{:S(2)}, u32[]{:S(2)}) collective-permute-start(bf16[32,2688]{1,0:T(8,128)(2,1)S(1)} %get-tuple-element.46), channel_id=1, source_target_pairs={{8,6},{9,7},{10,0},{11,1},{12,2},{13,3},{14,4},{15,5},{16,14},{17,... | collective-permute-start | bytes 516104 | tf_op jit(solution)/shard_map/ppermute | solution.py:325
  35.6 1.3 %collective-permute-start.8 = (bf16[32,2688]{1,0:T(8,128)(2,1)S(1)}, bf16[32,2688]{1,0:T(8,128)(2,1)S(1)}, u32[]{:S(2)}, u32[]{:S(2)}) collective-permute-start(bf16[32,2688]{1,0:T(8,128)(2,1)S(1)} %get-tuple-element.47), channel_id=1, source_target_pairs={{8,4},{9,5},{10,6},{11,7},{12,0},{13,1},{14,2},{15,3},{16,12},{17,... | collective-permute-start | bytes 516104 | tf_op jit(solution)/shard_map/ppermute | solution.py:325
  36.9 1.3 %collective-permute-start.9 = (bf16[32,2688]{1,0:T(8,128)(2,1)S(1)}, bf16[32,2688]{1,0:T(8,128)(2,1)S(1)}, u32[]{:S(2)}, u32[]{:S(2)}) collective-permute-start(bf16[32,2688]{1,0:T(8,128)(2,1)S(1)} %get-tuple-element.48), channel_id=1, source_target_pairs={{8,2},{9,3},{10,4},{11,5},{12,6},{13,7},{14,0},{15,1},{16,10},{17,... | collective-permute-start | bytes 516104 | tf_op jit(solution)/shard_map/ppermute | solution.py:325
  38.2 4.1 %shard_map.100 = bf16[264,4096]{1,0:T(8,128)(2,1)} custom-call(s32[2]{0:T(128)S(1)} %pad_add_fusion.me, bf16[264,4096]{1,0:T(8,128)(2,1)S(1)} %get-tuple-element.49.grad_ref), custom_call_target="tpu_custom_call" | custom-call | flops 570949632 | bytes 4325384 | tf_op jit(solution)/shard_map/pallas_call | solution.py:279
  42.3 0.0 collective-permute-done.6.refs_0_
  42.3 3.5 %collective-permute-done.7.refs_1_ = bf16[32,2688]{1,0:T(8,128)(2,1)S(1)} collective-permute-done((bf16[32,2688]{1,0:T(8,128)(2,1)S(1)}, bf16[32,2688]{1,0:T(8,128)(2,1)S(1)}, u32[]{:S(2)}, u32[]{:S(2)}) %collective-permute-start.7) | collective-permute-done | bytes 172064 | tf_op jit(solution)/shard_map/ppermute | solution.py:325
  45.9 3.2 %collective-permute-done.8.refs_2_ = bf16[32,2688]{1,0:T(8,128)(2,1)S(1)} collective-permute-done((bf16[32,2688]{1,0:T(8,128)(2,1)S(1)}, bf16[32,2688]{1,0:T(8,128)(2,1)S(1)}, u32[]{:S(2)}, u32[]{:S(2)}) %collective-permute-start.8) | collective-permute-done | bytes 172064 | tf_op jit(solution)/shard_map/ppermute | solution.py:325
  49.0 4.0 %collective-permute-done.9.refs_3_ = bf16[32,2688]{1,0:T(8,128)(2,1)S(1)} collective-permute-done((bf16[32,2688]{1,0:T(8,128)(2,1)S(1)}, bf16[32,2688]{1,0:T(8,128)(2,1)S(1)}, u32[]{:S(2)}, u32[]{:S(2)}) %collective-permute-start.9) | collective-permute-done | bytes 172064 | tf_op jit(solution)/shard_map/ppermute | solution.py:325
  53.0 1.3 %shard_map.99 = bf16[128,2560]{1,0:T(8,128)(2,1)} custom-call(bf16[32,2688]{1,0:T(8,128)(2,1)S(1)} %collective-permute-done.6.refs_0_, bf16[32,2688]{1,0:T(8,128)(2,1)S(1)} %collective-permute-done.7.refs_1_, bf16[32,2688]{1,0:T(8,128)(2,1)S(1)} %collective-permute-done.8.refs_2_, bf16[32,2688]{1,0:T(8,128)(2,1)S(1)} %collective-permute-done.9.refs_3_), custom_call_target="tpu_custom_call" | custom-call | flops 83886080 | bytes 1343488 | tf_op jit(solution)/shard_map/pallas_call | solution.py:279
  (2 shorter events, 0.1 us)
Async XLA Ops:
  2.9 14.8 %collective-permute-start = (bf16[32,2688]{1,0:T(8,128)(2,1)S(1)}, bf16[32,2688]{1,0:T(8,128)(2,1)S(1)}, u32[]{:S(2)}, u32[]{:S(2)}) collective-permute-start(bf16[32,2688]{1,0:T(8,128)(2,1)S(1)} %get-tuple-element.27), channel_id=1, source_target_pairs={{0,2},{1,3},{2,4},{3,5},{4,6},{5,7},{6,0},{7,1},{8,10},{9,11},{10,... | collective-permute-start | bytes 516104 | tf_op jit(solution)/shard_map/ppermute | solution.py:316
  5.8 11.9 %collective-permute-start.1 = (bf16[32,2688]{1,0:T(8,128)(2,1)S(1)}, bf16[32,2688]{1,0:T(8,128)(2,1)S(1)}, u32[]{:S(2)}, u32[]{:S(2)}) collective-permute-start(bf16[32,2688]{1,0:T(8,128)(2,1)S(1)} %get-tuple-element.28), channel_id=1, source_target_pairs={{0,4},{1,5},{2,6},{3,7},{4,0},{5,1},{6,2},{7,3},{8,12},{9,13},{10,... | collective-permute-start | bytes 516104 | tf_op jit(solution)/shard_map/ppermute | solution.py:316
  7.4 10.4 %collective-permute-start.2 = (bf16[32,2688]{1,0:T(8,128)(2,1)S(1)}, bf16[32,2688]{1,0:T(8,128)(2,1)S(1)}, u32[]{:S(2)}, u32[]{:S(2)}) collective-permute-start(bf16[32,2688]{1,0:T(8,128)(2,1)S(1)} %get-tuple-element.29), channel_id=1, source_target_pairs={{0,6},{1,7},{2,0},{3,1},{4,2},{5,3},{6,4},{7,5},{8,14},{9,15},{10,... | collective-permute-start | bytes 516104 | tf_op jit(solution)/shard_map/ppermute | solution.py:316
  8.8 11.2 %copy-start = (bf16[1,2560,4]{1,2,0:T(4,128)(2,1)S(1)}, bf16[1,2560,4]{1,2,0:T(4,128)(2,1)}, u32[]{:S(2)}) copy-start(bf16[1,2560,4]{1,2,0:T(4,128)(2,1)} %param.15) | copy-start | bytes 61444
  17.8 2.0 %collective-permute-start.4 = (bf16[96,2688]{1,0:T(8,128)(2,1)S(1)}, bf16[96,2688]{1,0:T(8,128)(2,1)S(1)}, u32[]{:S(2)}, u32[]{:S(2)}) collective-permute-start(bf16[96,2688]{1,0:T(8,128)(2,1)S(1)} %pad_maximum_fusion), channel_id=1, source_target_pairs={{0,1},{1,0},{2,3},{3,2},{4,5},{5,4},{6,7},{7,6},{8,9},{9,8},{10,11... | collective-permute-start | bytes 1548296 | tf_op jit(solution)/shard_map/ppermute | solution.py:316
  17.9 2.1 %collective-permute-start.3 = (bf16[32,2688]{1,0:T(8,128)(2,1)S(1)}, bf16[32,2688]{1,0:T(8,128)(2,1)S(1)}, u32[]{:S(2)}, u32[]{:S(2)}) collective-permute-start(bf16[32,2688]{1,0:T(8,128)(2,1)S(1)} %get-tuple-element.26.refs_0_.refs_1_), channel_id=1, source_target_pairs={{0,1},{1,0},{2,3},{3,2},{4,5},{5,4},{6,7},{7,6},{8,9},{9,8},{10,11... | collective-permute-start | bytes 516104 | tf_op jit(solution)/shard_map/ppermute | solution.py:316
  30.6 2.3 %collective-permute-start.5 = (bf16[144,2560]{1,0:T(8,128)(2,1)S(1)}, bf16[144,2560]{1,0:T(8,128)(2,1)S(1)}, u32[]{:S(2)}, u32[]{:S(2)}) collective-permute-start(bf16[144,2560]{1,0:T(8,128)(2,1)S(1)} %get-tuple-element.44), channel_id=1, source_target_pairs={{0,1},{1,0},{2,3},{3,2},{4,5},{5,4},{6,7},{7,6},{8,9},{9,8},{10,11... | collective-permute-start | bytes 2211848 | tf_op jit(solution)/shard_map/ppermute | solution.py:316
  33.0 9.3 %collective-permute-start.6 = (bf16[32,2688]{1,0:T(8,128)(2,1)S(1)}, bf16[32,2688]{1,0:T(8,128)(2,1)S(1)}, u32[]{:S(2)}, u32[]{:S(2)}) collective-permute-start(bf16[32,2688]{1,0:T(8,128)(2,1)S(1)} %get-tuple-element.45), channel_id=1, source_target_pairs={{8,0},{9,1},{10,2},{11,3},{12,4},{13,5},{14,6},{15,7},{16,8},{17,9... | collective-permute-start | bytes 516104 | tf_op jit(solution)/shard_map/ppermute | solution.py:325
  34.3 11.5 %collective-permute-start.7 = (bf16[32,2688]{1,0:T(8,128)(2,1)S(1)}, bf16[32,2688]{1,0:T(8,128)(2,1)S(1)}, u32[]{:S(2)}, u32[]{:S(2)}) collective-permute-start(bf16[32,2688]{1,0:T(8,128)(2,1)S(1)} %get-tuple-element.46), channel_id=1, source_target_pairs={{8,6},{9,7},{10,0},{11,1},{12,2},{13,3},{14,4},{15,5},{16,14},{17,... | collective-permute-start | bytes 516104 | tf_op jit(solution)/shard_map/ppermute | solution.py:325
  35.6 13.4 %collective-permute-start.8 = (bf16[32,2688]{1,0:T(8,128)(2,1)S(1)}, bf16[32,2688]{1,0:T(8,128)(2,1)S(1)}, u32[]{:S(2)}, u32[]{:S(2)}) collective-permute-start(bf16[32,2688]{1,0:T(8,128)(2,1)S(1)} %get-tuple-element.47), channel_id=1, source_target_pairs={{8,4},{9,5},{10,6},{11,7},{12,0},{13,1},{14,2},{15,3},{16,12},{17,... | collective-permute-start | bytes 516104 | tf_op jit(solution)/shard_map/ppermute | solution.py:325
  36.9 16.1 %collective-permute-start.9 = (bf16[32,2688]{1,0:T(8,128)(2,1)S(1)}, bf16[32,2688]{1,0:T(8,128)(2,1)S(1)}, u32[]{:S(2)}, u32[]{:S(2)}) collective-permute-start(bf16[32,2688]{1,0:T(8,128)(2,1)S(1)} %get-tuple-element.48), channel_id=1, source_target_pairs={{8,2},{9,3},{10,4},{11,5},{12,6},{13,7},{14,0},{15,1},{16,10},{17,... | collective-permute-start | bytes 516104 | tf_op jit(solution)/shard_map/ppermute | solution.py:325

commit v2 on v1

--- a/solution.py
+++ b/solution.py
@@ -75,8 +75,8 @@
     last_token = nt_dot((mine * number).astype(BF16), by_turn)
     copies[-1].wait()
     upstream = up_ref[...]
-    packed = dot(pick, upstream)
-    last_rows = dot(last.astype(BF16), upstream)
+    packed = dot(jnp.concatenate([pick, last.astype(BF16)], axis=0), upstream)
+    last_rows = packed[experts * main :]
     side_row = iota((main, LANES), 0)
     for k in range(experts):
         outs[k][:, :width] = packed[k * main : (k + 1) * main].astype(BF16)
@@ -103,31 +103,21 @@
     return jnp.where(slot < main, block * main + slot, total * main + block)
 
 
-def copies_of(source, first, targets, sems):
-    step = targets[0].shape[0]
-    return [
-        pltpu.make_async_copy(source.at[(first + i) * step : (first + i + 1) * step], target, sems.at[i])
-        for i, target in enumerate(targets)
-    ]
-
-
-def window_kernel(experts, group, main, chunks, me, kept_in, down_in, weight_in, out_ref, *refs):
-    downs, weights, refs = refs[: chunks[0]], refs[chunks[0] : -4], refs[-4:]
-    kept_ref, kept_sem, down_sems, weight_sems = refs
-    kept_copy = pltpu.make_async_copy(kept_in, kept_ref, kept_sem)
-    kept_copy.start()
-    copies = copies_of(down_in, 0, downs, down_sems) + copies_of(weight_in, 0, weights, weight_sems)
-    for copy in copies:
-        copy.start()
-    rows, columns = out_ref.shape
-    place = arrival_row(iota((1, rows), 1), me, experts, group, main, experts * group)
+def silu_parts(gate_value):
+    sigm = jax.nn.sigmoid(gate_value)
+    return (gate_value * sigm, sigm * (1.0 + gate_value * (1.0 - sigm)))
+
+
+def order_kernel(experts, group, main, me, gate_ref, up_ref, hidden_ref, gate_rate_ref, up_rate_ref):
+    rows = gate_ref.shape[0]
+    total = experts * group
+    place = arrival_row(iota((1, rows), 1), me, experts, group, main, total)
     pick = one_hot(iota((rows, rows), 0) == place)
-    kept_copy.wait()
-    step = min(1024, columns)
-    for c in range(0, columns, step):
-        out_ref[:, c : c + step] = dot(pick, kept_ref[:, c : c + step]).astype(BF16)
-    for copy in copies:
-        copy.wait()
+    activated, bend = silu_parts(dot(pick, gate_ref[...]))
+    up_value = dot(pick, up_ref[...])
+    hidden_ref[...] = (activated * up_value).astype(BF16)
+    gate_rate_ref[...] = up_value * bend
+    up_rate_ref[...] = activated
 
 
 def restore_kernel(experts, group, main, me, grad_ref, out_ref):
@@ -136,26 +126,16 @@
     out_ref[...] = dot(one_hot(iota((rows, rows), 1) == place), grad_ref[...]).astype(BF16)
 
 
-def silu_parts(gate_value):
-    sigm = jax.nn.sigmoid(gate_value)
-    return (gate_value * sigm, sigm * (1.0 + gate_value * (1.0 - sigm)))
-
-
-def expert_kernel(experts, group, main, chunks, fetched, me, *refs):
+def expert_kernel(experts, group, main, me, *refs):
     total = experts * group
     blocks, refs = refs[:total], refs[total:]
-    downs, refs = refs[: chunks[0]], refs[chunks[0] :]
-    weights, refs = refs[:fetched], refs[fetched:]
-    kept_ref, router_ref, weight_in, grad_ref, own_ref, last_ref = refs[:6]
-    sends, refs = refs[6 : 5 + group], refs[5 + group :]
-    late, (rows, raw_a, raw_b, late_sems) = refs[:-4], refs[-4:]
-    late_copies = copies_of(weight_in, fetched, late, late_sems)
-    for copy in late_copies:
-        copy.start()
+    hidden_ref, gate_rate_ref, up_rate_ref, router_ref, down_ref, weight_ref = refs[:6]
+    grad_ref, own_ref, last_ref = refs[6:9]
+    sends, (rows, raw_a, raw_b) = refs[9:-3], refs[-3:]
     raws = (raw_a, raw_b)
     count, width = rows.shape
     parts = width // LANES
-    half = kept_ref.shape[1] // 2
+    half = down_ref.shape[0]
     full, own = total * main, experts * main
 
     sides = []
@@ -168,83 +148,78 @@
     last = dot(one_hot(pick), sides)
     for c in range(parts):
         rows[full:, c * LANES : (c + 1) * LANES] = last[c * total : (c + 1) * total].astype(BF16)
-    row = iota((count, 1), 0)
-    block = jnp.where(row < full, row // main, row - full)
-    slot = jnp.where(row < full, lax.rem(row, main), main)
-    own_lane = iota((count, LANES), 1) == slot
-
-    def column(which):
-        choose = iota((count, full), 1) == block * main + parts + which
-        return jnp.sum(jnp.where(own_lane, dot(one_hot(choose), sides), 0.0), axis=1, keepdims=True)
-
-    score = column(SCORE)
-    slope = column(SLOPE_HIGH) + column(SLOPE_LOW)
+    def slot_columns():
+        row = iota((count, 1), 0)
+        block = jnp.where(row < full, row // main, row - full)
+        slot = jnp.where(row < full, lax.rem(row, main), main)
+        own_lane = iota((count, LANES), 1) == slot
+
+        def column(which):
+            choose = iota((count, full), 1) == block * main + parts + which
+            return jnp.sum(jnp.where(own_lane, dot(one_hot(choose), sides), 0.0), axis=1, keepdims=True)
+
+        return column(SCORE), column(SLOPE_HIGH) + column(SLOPE_LOW)
+
     step = raw_a.shape[1]
     inner = jnp.zeros((count, LANES), F32)
 
     def finish(start, raw, inner):
         piece, other = slice(start, start + step), slice(half + start, half + start + step)
-        up_value = kept_ref[:, other].astype(F32)
-        activated, bend = silu_parts(kept_ref[:, piece].astype(F32))
-        hidden = (activated * up_value).astype(BF16).astype(F32)
         hidden_grad = score * raw
-        grad_ref[:, piece] = (hidden_grad * up_value * bend).astype(BF16)
-        grad_ref[:, other] = (hidden_grad * activated).astype(BF16)
-        product = hidden * raw
+        grad_ref[:, piece] = (hidden_grad * gate_rate_ref[:, piece]).astype(BF16)
+        grad_ref[:, other] = (hidden_grad * up_rate_ref[:, piece]).astype(BF16)
+        product = hidden_ref[:, piece].astype(F32) * raw
         return inner + sum(product[:, c : c + LANES] for c in range(0, step, LANES))
 
     for i in range(half // step):
-        raws[i % 2][...] = nt_dot(rows[...], downs[i][...])
-        if i:
+        raws[i % 2][...] = nt_dot(rows[...], down_ref[i * step : (i + 1) * step, :])
+        if i == 0:
+            score, slope = slot_columns()
+        else:
             inner = finish((i - 1) * step, raws[(i - 1) % 2][...], inner)
     inner = finish(half - step, raws[(half // step - 1) % 2][...], inner)
     coeff = slope * jnp.sum(inner, axis=1, keepdims=True)
 
-    step = late[0].shape[0]
-    for i, weight_ref in enumerate(list(weights) + list(late)):
-        if i >= fetched:
-            late_copies[i - fetched].wait()
-        piece = slice(i * step, (i + 1) * step)
+    step = 512 if width % 512 == 0 else LANES
+    for start in range(0, width, step):
+        piece = slice(start, start + step)
         router = router_ref[:, piece].astype(F32)
         router = sum(jnp.where(me[0] == e, router[e : e + 1], 0.0) for e in range(experts))
-        partial = nt_dot(grad_ref[...], weight_ref[...]) + coeff * router
+        partial = nt_dot(grad_ref[...], weight_ref[piece, :]) + coeff * router
         last = partial[full:]
         own_ref[:, piece] = partial[:own]
         last_ref[:, piece] = last
         for lane in range(1, group):
-            out = sends[lane - 1]
-            out[:own, piece] = partial[lane * own : (lane + 1) * own].astype(BF16)
-            out[own : own + total, piece] = last.astype(BF16)
-            if out.shape[0] > own + total:
-                out[own + total :, piece] = jnp.zeros((out.shape[0] - own - total, step), BF16)
-
-
-def merge_kernel(experts, group, main, own_ref, last_ref, *refs):
-    others = refs[: group - 1]
-    sides = refs[group - 1 : group - 1 + experts]
-    outs = refs[group - 1 + experts :]
+            for k in range(experts):
+                out = sends[(lane - 1) * experts + k]
+                first = lane * own + k * main
+                out[:main, piece] = partial[first : first + main].astype(BF16)
+                if k == 0:
+                    out[main : main + total, piece] = last.astype(BF16)
+                    if out.shape[0] > main + total:
+                        out[main + total :, piece] = jnp.zeros((out.shape[0] - main - total, step), BF16)
+
+
+def merge_kernel(experts, group, main, k, own_ref, last_ref, side_ref, *refs):
+    others, firsts, out_ref = refs[: group - 1], refs[group - 1 : -1], refs[-1]
     width = own_ref.shape[1]
-    parts = width // LANES
-    own = experts * main
     total = experts * group
-    lasts = [other[own : own + total, :].astype(F32) for other in others]
+    value = own_ref[k * main : (k + 1) * main, :]
+    last = last_ref[k : k + 1, :]
+    for lane, (other, first) in enumerate(zip(others, firsts), 1):
+        value += other[:main, :].astype(F32)
+        row = lane * experts + k
+        last += first[main : main + total, :].astype(F32)[row : row + 1]
+    out_ref[:, :width] = value.astype(BF16)
+    side = side_ref[:, width:].astype(F32)
     side_row = iota((main, LANES), 0)
-    for k in range(experts):
-        value = own_ref[k * main : (k + 1) * main, :]
-        last = last_ref[k : k + 1, :]
-        for lane, other in enumerate(others, 1):
-            value += other[k * main : (k + 1) * main, :].astype(F32)
-            row = lane * experts + k
-            last += lasts[lane - 1][row : row + 1, :]
-        outs[k][:, :width] = value.astype(BF16)
-        side = sides[k][:, width:].astype(F32)
-        for c in range(parts):
-            side = jnp.where(side_row == c, last[:, c * LANES : (c + 1) * LANES], side)
-        outs[k][:, width:] = side.astype(BF16)
+    for c in range(width // LANES):
+        side = jnp.where(side_row == c, last[:, c * LANES : (c + 1) * LANES], side)
+    out_ref[:, width:] = side.astype(BF16)
 
 
 def tokens_kernel(experts, main, *refs):
-    blocks, (out_ref, rows) = refs[:experts], refs[experts:]
+    blocks, (out, rows, out_ref, sems) = refs[:experts], refs[experts:]
     tokens, width = out_ref.shape
     parts = width // LANES
     sides = []
@@ -267,7 +242,19 @@
     main_pick = (number == token).astype(F32).astype(BF16)
     last_pick = (number == last_token).astype(F32).astype(BF16)
     pick = jnp.concatenate([main_pick[:, : experts * main], last_pick[:, :height]], axis=1)
-    out_ref[...] = dot(pick, rows[...]).astype(BF16)
+    step = width // sems.shape[0]
+    copies = []
+    for i in range(sems.shape[0]):
+        piece = slice(i * step, (i + 1) * step)
+        out_ref[:, piece] = dot(pick, rows[:, piece]).astype(BF16)
+        copies.append(pltpu.make_async_copy(out_ref.at[:, piece], out.at[:, piece], sems.at[i]))
+        copies[-1].start()
+    for copy in copies:
+        copy.wait()
+
+
+PACK_FLOPS = 20 * 10**9
+ORDER_FLOPS = 2 * 10**9
 
 
 def call(kernel, outs, ins, flops=0, limit=4, **options):
@@ -328,7 +315,7 @@
         functools.partial(pack_kernel, experts, main),
         [block] * experts,
         [me, out_grad[0], expert_ids, slot_ids, router_logits[0].T],
-        2 * own * tokens * width,
+        PACK_FLOPS,
         in_specs=[SMEM] + [HBM] * 4,
         out_specs=[VMEM] * experts,
         scratch_shapes=[
@@ -342,68 +329,64 @@
     held = [packed[0]] + [send(packed[k], k, 0) for k in range(1, experts)]
     first = [send(packed[0], 0, lane) for lane in range(1, group)]
 
-    chunks = (max(1, half // 512), max(1, width // 512))
-    fetched = chunks[1] - 2
-    down_shape, weight_shape = (half // chunks[0], width), (width // chunks[1], 2 * half)
-    ordered, *weights = call(
-        functools.partial(window_kernel, experts, group, main, chunks),
-        [shape(capacity, 2 * half)]
-        + [pltpu.VMEM(down_shape, BF16)] * chunks[0]
-        + [pltpu.VMEM(weight_shape, BF16)] * fetched,
-        [me, saved_routed[0, 0], w_down[0, 0], w_gate_up[0, 0]],
-        2 * capacity * capacity * 2 * half,
-        8,
-        in_specs=[SMEM] + [HBM] * 3,
-        out_specs=[VMEM] * (1 + chunks[0] + fetched),
-        scratch_shapes=[
-            pltpu.VMEM((capacity, 2 * half), BF16),
-            pltpu.SemaphoreType.DMA,
-            pltpu.SemaphoreType.DMA((chunks[0],)),
-            pltpu.SemaphoreType.DMA((fetched,)),
-        ],
-    )
-    held[1:], ordered = lax.optimization_barrier((held[1:], ordered))
+    columns = min(256, half)
+    tile = pl.BlockSpec((capacity, columns), lambda i: (0, i))
+    hidden, gate_rate, up_rate = call(
+        functools.partial(order_kernel, experts, group, main),
+        [shape(capacity, half)] + [shape(capacity, half, dtype=F32)] * 2,
+        [me, saved_routed[0, 0], saved_routed[0, 0]],
+        ORDER_FLOPS,
+        3 + capacity * columns * 36 // 2**20,
+        grid=(half // columns,),
+        in_specs=[SMEM, tile, pl.BlockSpec((capacity, columns), lambda i: (0, i + half // columns))],
+        out_specs=[tile] * 3,
+    )
     arrived = list(held)
-    rest = jnp.concatenate(held[1:], axis=0)
     for lane in range(1, group):
-        other = send(rest, 0, lane)
         arrived.append(first[lane - 1])
-        arrived += [other[k * main : (k + 1) * main] for k in range(experts - 1)]
-
-    padded = own + -(-total // 16) * 16
-    scratch = [pltpu.VMEM(weight_shape, BF16)] * (chunks[1] - fetched) + [
+        for k in range(1, experts):
+            value, hidden = lax.optimization_barrier((held[k], hidden))
+            arrived.append(send(value, 0, lane))
+
+    padded = main + -(-total // 16) * 16
+    sent_shapes = [shape(padded, width)] + [shape(main, width)] * (experts - 1)
+    step = min(256, half)
+    scratch = [
         pltpu.VMEM((capacity, width), BF16),
-        pltpu.VMEM((capacity, down_shape[0]), F32),
-        pltpu.VMEM((capacity, down_shape[0]), F32),
+        pltpu.VMEM((capacity, step), F32),
+        pltpu.VMEM((capacity, step), F32),
     ]
     grads, own_part, last_part, *sent = call(
-        functools.partial(expert_kernel, experts, group, main, chunks, fetched),
+        functools.partial(expert_kernel, experts, group, main),
         [
             shape(capacity, 2 * half),
             shape(own, width, dtype=F32),
             shape(total, width, dtype=F32),
         ]
-        + [shape(padded, width)] * (group - 1),
-        [me, *arrived]
-        + [pltpu.with_memory_space_constraint(x, pltpu.VMEM) for x in weights]
-        + [ordered, w_router[0].T, w_gate_up[0, 0]],
+        + sent_shapes * (group - 1),
+        [me, *arrived, hidden, gate_rate, up_rate, w_router[0].T]
+        + [pltpu.with_memory_space_constraint(x[0, 0], pltpu.VMEM) for x in (w_down, w_gate_up)],
         6 * capacity * width * half,
         grant(scratch, 6),
-        in_specs=[SMEM] + [VMEM] * (total + 2 + chunks[0] + fetched) + [HBM],
-        out_specs=[VMEM] * (2 + group),
-        scratch_shapes=scratch + [pltpu.SemaphoreType.DMA((chunks[1] - fetched,))],
-    )
-    others = [send(sent[lane - 1], 0, -lane) for lane in range(1, group)]
-
-    merged = call(
-        functools.partial(merge_kernel, experts, group, main),
-        [block] * experts,
-        [own_part, last_part] + others + held,
-        own * width * group,
-        in_specs=[VMEM] * (1 + group + experts),
-        out_specs=[VMEM] * experts,
-    )
-    returned = [send_back(merged[k], k) for k in range(experts)]
+        in_specs=[SMEM] + [VMEM] * (total + 6),
+        out_specs=[VMEM] * (3 + (group - 1) * experts),
+        scratch_shapes=scratch,
+    )
+    others = [
+        [send(sent[(lane - 1) * experts + k], 0, -lane) for lane in range(1, group)]
+        for k in range(experts)
+    ]
+    returned = []
+    for k in range(experts):
+        (merged,) = call(
+            functools.partial(merge_kernel, experts, group, main, k),
+            [block],
+            [own_part, last_part, held[k], *others[k], *others[0]],
+            main * width * group,
+            in_specs=[VMEM] * (1 + 2 * group),
+            out_specs=[VMEM],
+        )
+        returned.append(send_back(merged, k))
 
     columns = min(1024, 2 * half)
     (hidden_grads,) = call(
@@ -418,12 +401,16 @@
     )
     (previous,) = call(
         functools.partial(tokens_kernel, experts, main),
-        [shape(tokens, width)],
+        [pltpu.HBM((tokens, width), BF16)],
         returned,
         2 * own * tokens * width,
         in_specs=[VMEM] * experts,
-        out_specs=[VMEM],
-        scratch_shapes=[pltpu.VMEM((own + 16, width), BF16)],
+        out_specs=[HBM],
+        scratch_shapes=[
+            pltpu.VMEM((own + 16, width), BF16),
+            pltpu.VMEM((tokens, width), BF16),
+            pltpu.SemaphoreType.DMA((4 if width % (4 * LANES) == 0 else 1,)),
+        ],
     )
     return (previous[None], hidden_grads[None, None])
 

time: 54.6 us -> 51.6 us (0.945)
  Pallas kernels: 27.2 us -> 21.9 us
  waiting for transfers between devices: 14.4 us -> 15.7 us
  starting transfers between devices: 11.9 us -> 12.7 us
    pallas_call x6 -> x9, Pallas kernels: 27.2 us -> 21.9 us  [call(): pl.pallas_call(kernel, out_shape=tuple(outs), cost_estimate=pl.CostEstima...]
    ppermute x4, waiting for transfers between devices: 10.7 us -> 11.7 us  [send_back(): return lax.ppermute(value, ('section', 'expert'), pairs)]
    ppermute x6 -> x11, starting transfers between devices: 6.71 us -> 7.54 us  [send(): return lax.ppermute(value, 'expert', pairs)]
    ppermute x6 -> x11, waiting for transfers between devices: 3.68 us -> 4.08 us  [send(): return lax.ppermute(value, 'expert', pairs)]
  transfers between devices with their start and end apart: 10 -> 15, of which waited for: 6 -> 9; matrix products, arithmetic and copies ran while one was open for 0% -> 0% of each run, Pallas kernels for 24% -> 16%
where the time goes in v2:
time: 51.6 us; the launch traced here: 51.4 us
  Pallas kernels  21.9 us (42%)
  waiting for transfers between devices  15.7 us (30%)
  starting transfers between devices  12.7 us (25%)
  between operations  0.87 us (2%)
    pallas_call x9, Pallas kernels, call(): pl.pallas_call(kernel, out_shape=tuple(outs), cost_estimate=pl.CostEstima...  21.9 us
    ppermute x4, waiting for transfers between devices, send_back(): return lax.ppermute(value, ('section', 'expert'), pairs)  11.7 us
    ppermute x11, starting transfers between devices, send(): return lax.ppermute(value, 'expert', pairs)  7.54 us
    ppermute x4, starting transfers between devices, send_back(): return lax.ppermute(value, ('section', 'expert'), pairs)  5.17 us
    ppermute x11, waiting for transfers between devices, send(): return lax.ppermute(value, 'expert', pairs)  4.08 us
  transfers between devices with their start and end apart: 15, of which 9 were waited for; matrix products, arithmetic and copies ran while one was open for 0% of the time, Pallas kernels for 16%

profile of v2, /device:TPU:0, one launch (start us, length us, event | category | flops | bytes accessed | tf_op | source)
XLA Modules:
  0.0 51.4 jit_solution(18255625118069568533)
XLA Ops:
  0.6 0.1 pad_add_fusion.me
  0.7 0.0 slice-start.2
  0.8 2.2 %shard_map.95 = (bf16[32,2688]{1,0:T(8,128)(2,1)S(1)}, bf16[32,2688]{1,0:T(8,128)(2,1)S(1)}, bf16[32,2688]{1,0:T(8,128)(2,1)S(1)}, bf16[32,2688]{1,0:T(8,128)(2,1)S(1)}) custom-call(s32[2]{0:T(128)S(1)} %pad_add_fusion.me, bf16[128,2560]{1,0:T(8,128)(2,1)} %bitcast.25, s32[1,128]{1,0:T(1,128)} %route_in.1, s32[1,128]{1,0:T(1,128)} %slot_in.1, f32[4,128]{1,0:T(4,128)} %bitcast.26), custom_call_target="tpu_custom_call" | custom-call | flops 20000000000 | bytes 1346568 | tf_op jit(solution)/shard_map/pallas_call | solution.py:266
  3.0 3.0 %collective-permute-start = (bf16[32,2688]{1,0:T(8,128)(2,1)S(1)}, bf16[32,2688]{1,0:T(8,128)(2,1)S(1)}, u32[]{:S(2)}, u32[]{:S(2)}) collective-permute-start(bf16[32,2688]{1,0:T(8,128)(2,1)S(1)} %get-tuple-element.23), channel_id=1, source_target_pairs={{0,2},{1,3},{2,4},{3,5},{4,6},{5,7},{6,0},{7,1},{8,10},{9,11},{10,... | collective-permute-start | bytes 516104 | tf_op jit(solution)/shard_map/ppermute | solution.py:303
  6.0 1.5 %collective-permute-start.1 = (bf16[32,2688]{1,0:T(8,128)(2,1)S(1)}, bf16[32,2688]{1,0:T(8,128)(2,1)S(1)}, u32[]{:S(2)}, u32[]{:S(2)}) collective-permute-start(bf16[32,2688]{1,0:T(8,128)(2,1)S(1)} %get-tuple-element.24), channel_id=1, source_target_pairs={{0,4},{1,5},{2,6},{3,7},{4,0},{5,1},{6,2},{7,3},{8,12},{9,13},{10,... | collective-permute-start | bytes 516104 | tf_op jit(solution)/shard_map/ppermute | solution.py:303
  7.5 1.4 %collective-permute-start.2 = (bf16[32,2688]{1,0:T(8,128)(2,1)S(1)}, bf16[32,2688]{1,0:T(8,128)(2,1)S(1)}, u32[]{:S(2)}, u32[]{:S(2)}) collective-permute-start(bf16[32,2688]{1,0:T(8,128)(2,1)S(1)} %get-tuple-element.25), channel_id=1, source_target_pairs={{0,6},{1,7},{2,0},{3,1},{4,2},{5,3},{6,4},{7,5},{8,14},{9,15},{10,... | collective-permute-start | bytes 516104 | tf_op jit(solution)/shard_map/ppermute | solution.py:303
  9.0 4.2 %shard_map.96 = (bf16[264,2048]{1,0:T(8,128)(2,1)S(1)}, f32[264,2048]{1,0:T(8,128)S(1)}, f32[264,2048]{1,0:T(8,128)S(1)}) custom-call(s32[2]{0:T(128)S(1)} %pad_add_fusion.me, bf16[264,4096]{1,0:T(8,128)(2,1)S(1)} %bitcast.21, bf16[264,4096]{1,0:T(8,128)(2,1)S(1)} %bitcast.22), custom_call_target="tpu_custom_call" | custom-call | flops 2000000000 | bytes 9732104 | tf_op jit(solution)/shard_map/pallas_call | solution.py:266
  13.2 1.9 %collective-permute-done.1.refs_2_.side_ref = bf16[32,2688]{1,0:T(8,128)(2,1)S(1)} collective-permute-done((bf16[32,2688]{1,0:T(8,128)(2,1)S(1)}, bf16[32,2688]{1,0:T(8,128)(2,1)S(1)}, u32[]{:S(2)}, u32[]{:S(2)}) %collective-permute-start.1) | collective-permute-done | bytes 172064 | tf_op jit(solution)/shard_map/ppermute | solution.py:303
  15.1 0.3 collective-permute-done.2.refs_3_.side_ref
  15.3 0.5 collective-permute-start.5
  15.9 0.0 collective-permute-start.4
  15.9 0.9 %collective-permute-done.6.refs_7_ = bf16[32,2688]{1,0:T(8,128)(2,1)S(1)} collective-permute-done((bf16[32,2688]{1,0:T(8,128)(2,1)S(1)}, bf16[32,2688]{1,0:T(8,128)(2,1)S(1)}, u32[]{:S(2)}, u32[]{:S(2)}) %collective-permute-start.6) | collective-permute-done | bytes 172064 | tf_op jit(solution)/shard_map/ppermute | solution.py:303
  16.7 0.2 collective-permute-done.5.refs_6_
  17.0 0.3 collective-permute-done.4.refs_5_
  17.3 10.0 %shard_map.97 = (bf16[264,4096]{1,0:T(8,128)(2,1)S(1)}, f32[128,2560]{1,0:T(8,128)S(1)}, f32[8,2560]{1,0:T(8,128)S(1)}, bf16[48,2560]{1,0:T(8,128)(2,1)S(1)}, bf...) custom-call(s32[2]{0:T(128)S(1)} %pad_add_fusion.me, ...), custom_call_target="tpu_custom_call" | custom-call | flops 8304721920 | bytes 42553352 | tf_op jit(solution)/shard_map/pallas_call | solution.py:266
  27.3 0.3 collective-permute-start.7
  27.6 0.3 collective-permute-start.9
  27.9 0.2 collective-permute-start.11
  28.2 0.3 collective-permute-start.13
  28.4 0.5 collective-permute-done.7.refs_0_.refs_1_
  29.0 1.3 %collective-permute-start.8 = (bf16[32,2688]{1,0:T(8,128)(2,1)S(1)}, bf16[32,2688]{1,0:T(8,128)(2,1)S(1)}, u32[]{:S(2)}, u32[]{:S(2)}) collective-permute-start(bf16[32,2688]{1,0:T(8,128)(2,1)S(1)} %shard_map.98), channel_id=1, source_target_pairs={{8,0},{9,1},{10,2},{11,3},{12,4},{13,5},{14,6},{15,7},{16,8},{17,9... | collective-permute-start | bytes 516104 | tf_op jit(solution)/shard_map/ppermute | solution.py:312
  30.3 0.1 shard_map.99
  30.3 1.3 %collective-permute-start.10 = (bf16[32,2688]{1,0:T(8,128)(2,1)S(1)}, bf16[32,2688]{1,0:T(8,128)(2,1)S(1)}, u32[]{:S(2)}, u32[]{:S(2)}) collective-permute-start(bf16[32,2688]{1,0:T(8,128)(2,1)S(1)} %shard_map.99), channel_id=1, source_target_pairs={{8,6},{9,7},{10,0},{11,1},{12,2},{13,3},{14,4},{15,5},{16,14},{17,... | collective-permute-start | bytes 516104 | tf_op jit(solution)/shard_map/ppermute | solution.py:312
  31.6 0.1 shard_map.100
  31.7 1.3 %collective-permute-start.12 = (bf16[32,2688]{1,0:T(8,128)(2,1)S(1)}, bf16[32,2688]{1,0:T(8,128)(2,1)S(1)}, u32[]{:S(2)}, u32[]{:S(2)}) collective-permute-start(bf16[32,2688]{1,0:T(8,128)(2,1)S(1)} %shard_map.100), channel_id=1, source_target_pairs={{8,4},{9,5},{10,6},{11,7},{12,0},{13,1},{14,2},{15,3},{16,12},{17,... | collective-permute-start | bytes 516104 | tf_op jit(solution)/shard_map/ppermute | solution.py:312
  33.0 0.1 shard_map.101
  33.1 1.3 %collective-permute-start.14 = (bf16[32,2688]{1,0:T(8,128)(2,1)S(1)}, bf16[32,2688]{1,0:T(8,128)(2,1)S(1)}, u32[]{:S(2)}, u32[]{:S(2)}) collective-permute-start(bf16[32,2688]{1,0:T(8,128)(2,1)S(1)} %shard_map.101), channel_id=1, source_target_pairs={{8,2},{9,3},{10,4},{11,5},{12,6},{13,7},{14,0},{15,1},{16,10},{17,... | collective-permute-start | bytes 516104 | tf_op jit(solution)/shard_map/ppermute | solution.py:312
  34.4 4.1 %shard_map.103 = bf16[264,4096]{1,0:T(8,128)(2,1)} custom-call(s32[2]{0:T(128)S(1)} %pad_add_fusion.me, bf16[264,4096]{1,0:T(8,128)(2,1)S(1)} %get-tuple-element.41.grad_ref), custom_call_target="tpu_custom_call" | custom-call | flops 570949632 | bytes 4325384 | tf_op jit(solution)/shard_map/pallas_call | solution.py:266
  38.5 4.4 %collective-permute-done.10.refs_1_ = bf16[32,2688]{1,0:T(8,128)(2,1)S(1)} collective-permute-done((bf16[32,2688]{1,0:T(8,128)(2,1)S(1)}, bf16[32,2688]{1,0:T(8,128)(2,1)S(1)}, u32[]{:S(2)}, u32[]{:S(2)}) %collective-permute-start.10) | collective-permute-done | bytes 172064 | tf_op jit(solution)/shard_map/ppermute | solution.py:312
  42.9 3.4 %collective-permute-done.12.refs_2_ = bf16[32,2688]{1,0:T(8,128)(2,1)S(1)} collective-permute-done((bf16[32,2688]{1,0:T(8,128)(2,1)S(1)}, bf16[32,2688]{1,0:T(8,128)(2,1)S(1)}, u32[]{:S(2)}, u32[]{:S(2)}) %collective-permute-start.12) | collective-permute-done | bytes 172064 | tf_op jit(solution)/shard_map/ppermute | solution.py:312
  46.3 3.8 %collective-permute-done.14.refs_3_ = bf16[32,2688]{1,0:T(8,128)(2,1)S(1)} collective-permute-done((bf16[32,2688]{1,0:T(8,128)(2,1)S(1)}, bf16[32,2688]{1,0:T(8,128)(2,1)S(1)}, u32[]{:S(2)}, u32[]{:S(2)}) %collective-permute-start.14) | collective-permute-done | bytes 172064 | tf_op jit(solution)/shard_map/ppermute | solution.py:312
  50.1 1.2 %shard_map.102 = bf16[128,2560]{1,0:T(8,128)(2,1)} custom-call(bf16[32,2688]{1,0:T(8,128)(2,1)S(1)} %collective-permute-done.8.refs_0_, bf16[32,2688]{1,0:T(8,128)(2,1)S(1)} %collective-permute-done.10.refs_1_, bf16[32,2688]{1,0:T(8,128)(2,1)S(1)} %collective-permute-done.12.refs_2_, bf16[32,2688]{1,0:T(8,128)(2,1)S(1)} %collective-permute-done.14.refs_3_), custom_call_target="tpu_custom_call" | custom-call | flops 83886080 | bytes 1343488 | tf_op jit(solution)/shard_map/pallas_call | solution.py:266
  (30 shorter events, 0.1 us)
Async XLA Ops:
  0.7 16.5 %slice-start = ((s8[20971520]{0:T(1024)(128)(4,1)}), s8[4194304]{0:T(1024)(128)(4,1)S(1)}, s32[]{:S(2)}) async-start(s8[20971520]{0:T(1024)(128)(4,1)} %bitcast.14), calls=%async_computation | async-start | bytes 8388608
  0.7 16.5 %slice-start.5 = ((s8[10485760]{0:T(1024)(128)(4,1)}), s8[4194304]{0:T(1024)(128)(4,1)S(1)}, s32[]{:S(2)}) async-start(s8[10485760]{0:T(1024)(128)(4,1)} %bitcast.17), calls=%async_computation.5 | async-start | bytes 8388608
  0.7 8.3 %copy-start.1 = (bf16[1,1,264,4096]{3,2,1,0:T(8,128)(2,1)S(1)}, bf16[1,1,264,4096]{3,2,1,0:T(8,128)(2,1)}, u32[]{:S(2)}) copy-start(bf16[1,1,264,4096]{3,2,1,0:T(8,128)(2,1)} %param.12) | copy-start | bytes 6488068
  0.7 16.5 %slice-start.1 = ((s8[20971520]{0:T(1024)(128)(4,1)}), s8[4194304]{0:T(1024)(128)(4,1)S(1)}, s32[]{:S(2)}) async-start(s8[20971520]{0:T(1024)(128)(4,1)} %bitcast.14), calls=%async_computation.1 | async-start | bytes 8388608
  0.7 16.5 %slice-start.2 = ((s8[20971520]{0:T(1024)(128)(4,1)}), s8[4194304]{0:T(1024)(128)(4,1)S(1)}, s32[]{:S(2)}) async-start(s8[20971520]{0:T(1024)(128)(4,1)} %bitcast.14), calls=%async_computation.2 | async-start | bytes 8388608
  0.7 16.5 %slice-start.3 = ((s8[20971520]{0:T(1024)(128)(4,1)}), s8[4194304]{0:T(1024)(128)(4,1)S(1)}, s32[]{:S(2)}) async-start(s8[20971520]{0:T(1024)(128)(4,1)} %bitcast.14), calls=%async_computation.3 | async-start | bytes 8388608
  0.8 16.5 %slice-start.4 = ((s8[20971520]{0:T(1024)(128)(4,1)}), s8[4194304]{0:T(1024)(128)(4,1)S(1)}, s32[]{:S(2)}) async-start(s8[20971520]{0:T(1024)(128)(4,1)} %bitcast.14), calls=%async_computation.4 | async-start | bytes 8388608
  0.8 16.5 %slice-start.6 = ((s8[10485760]{0:T(1024)(128)(4,1)}), s8[4194304]{0:T(1024)(128)(4,1)S(1)}, s32[]{:S(2)}) async-start(s8[10485760]{0:T(1024)(128)(4,1)} %bitcast.17), calls=%async_computation.6 | async-start | bytes 8388608
  0.8 16.5 %slice-start.7 = ((s8[10485760]{0:T(1024)(128)(4,1)}), s8[2097152]{0:T(1024)(128)(4,1)S(1)}, s32[]{:S(2)}) async-start(s8[10485760]{0:T(1024)(128)(4,1)} %bitcast.17), calls=%async_computation.7 | async-start | bytes 4194304
  3.0 10.1 %collective-permute-start = (bf16[32,2688]{1,0:T(8,128)(2,1)S(1)}, bf16[32,2688]{1,0:T(8,128)(2,1)S(1)}, u32[]{:S(2)}, u32[]{:S(2)}) collective-permute-start(bf16[32,2688]{1,0:T(8,128)(2,1)S(1)} %get-tuple-element.23), channel_id=1, source_target_pairs={{0,2},{1,3},{2,4},{3,5},{4,6},{5,7},{6,0},{7,1},{8,10},{9,11},{10,... | collective-permute-start | bytes 516104 | tf_op jit(solution)/shard_map/ppermute | solution.py:303
  6.0 9.0 %collective-permute-start.1 = (bf16[32,2688]{1,0:T(8,128)(2,1)S(1)}, bf16[32,2688]{1,0:T(8,128)(2,1)S(1)}, u32[]{:S(2)}, u32[]{:S(2)}) collective-permute-start(bf16[32,2688]{1,0:T(8,128)(2,1)S(1)} %get-tuple-element.24), channel_id=1, source_target_pairs={{0,4},{1,5},{2,6},{3,7},{4,0},{5,1},{6,2},{7,3},{8,12},{9,13},{10,... | collective-permute-start | bytes 516104 | tf_op jit(solution)/shard_map/ppermute | solution.py:303
  7.5 7.8 %collective-permute-start.2 = (bf16[32,2688]{1,0:T(8,128)(2,1)S(1)}, bf16[32,2688]{1,0:T(8,128)(2,1)S(1)}, u32[]{:S(2)}, u32[]{:S(2)}) collective-permute-start(bf16[32,2688]{1,0:T(8,128)(2,1)S(1)} %get-tuple-element.25), channel_id=1, source_target_pairs={{0,6},{1,7},{2,0},{3,1},{4,2},{5,3},{6,4},{7,5},{8,14},{9,15},{10,... | collective-permute-start | bytes 516104 | tf_op jit(solution)/shard_map/ppermute | solution.py:303
  9.0 6.9 %collective-permute-start.3 = (bf16[32,2688]{1,0:T(8,128)(2,1)S(1)}, bf16[32,2688]{1,0:T(8,128)(2,1)S(1)}, u32[]{:S(2)}, u32[]{:S(2)}) collective-permute-start(bf16[32,2688]{1,0:T(8,128)(2,1)S(1)} %get-tuple-element.22.refs_0_.side_ref), channel_id=1, source_target_pairs={{0,1},{1,0},{2,3},{3,2},{4,5},{5,4},{6,7},{7,6},{8,9},{9,8},{10,11... | collective-permute-start | bytes 516104 | tf_op jit(solution)/shard_map/ppermute | solution.py:303
  9.0 8.3 %copy-start = (bf16[1,2560,4]{1,2,0:T(4,128)(2,1)S(1)}, bf16[1,2560,4]{1,2,0:T(4,128)(2,1)}, u32[]{:S(2)}) copy-start(bf16[1,2560,4]{1,2,0:T(4,128)(2,1)} %param.15) | copy-start | bytes 61444
  15.3 1.4 %collective-permute-start.6 = (bf16[32,2688]{1,0:T(8,128)(2,1)S(1)}, bf16[32,2688]{1,0:T(8,128)(2,1)S(1)}, u32[]{:S(2)}, u32[]{:S(2)}) collective-permute-start(bf16[32,2688]{1,0:T(8,128)(2,1)S(1)} %collective-permute-done.2.refs_3_.side_ref), channel_id=1, source_target_pairs={{0,1},{1,0},{2,3},{3,2},{4,5},{5,4},{6,7},{7,6},{8,9},{9,8},{10,11... | collective-permute-start | bytes 516104 | tf_op jit(solution)/shard_map/ppermute | solution.py:303
  15.3 1.6 %collective-permute-start.5 = (bf16[32,2688]{1,0:T(8,128)(2,1)S(1)}, bf16[32,2688]{1,0:T(8,128)(2,1)S(1)}, u32[]{:S(2)}, u32[]{:S(2)}) collective-permute-start(bf16[32,2688]{1,0:T(8,128)(2,1)S(1)} %collective-permute-done.1.refs_2_.side_ref), channel_id=1, source_target_pairs={{0,1},{1,0},{2,3},{3,2},{4,5},{5,4},{6,7},{7,6},{8,9},{9,8},{10,11... | collective-permute-start | bytes 516104 | tf_op jit(solution)/shard_map/ppermute | solution.py:303
  15.9 1.4 %collective-permute-start.4 = (bf16[32,2688]{1,0:T(8,128)(2,1)S(1)}, bf16[32,2688]{1,0:T(8,128)(2,1)S(1)}, u32[]{:S(2)}, u32[]{:S(2)}) collective-permute-start(bf16[32,2688]{1,0:T(8,128)(2,1)S(1)} %collective-permute-done.refs_1_.side_ref), channel_id=1, source_target_pairs={{0,1},{1,0},{2,3},{3,2},{4,5},{5,4},{6,7},{7,6},{8,9},{9,8},{10,11... | collective-permute-start | bytes 516104 | tf_op jit(solution)/shard_map/ppermute | solution.py:303
  27.3 1.6 %collective-permute-start.7 = (bf16[48,2560]{1,0:T(8,128)(2,1)S(1)}, bf16[48,2560]{1,0:T(8,128)(2,1)S(1)}, u32[]{:S(2)}, u32[]{:S(2)}) collective-permute-start(bf16[48,2560]{1,0:T(8,128)(2,1)S(1)} %get-tuple-element.37), channel_id=1, source_target_pairs={{0,1},{1,0},{2,3},{3,2},{4,5},{5,4},{6,7},{7,6},{8,9},{9,8},{10,11... | collective-permute-start | bytes 737288 | tf_op jit(solution)/shard_map/ppermute | solution.py:303
  27.6 2.6 %collective-permute-start.9 = (bf16[32,2560]{1,0:T(8,128)(2,1)S(1)}, bf16[32,2560]{1,0:T(8,128)(2,1)S(1)}, u32[]{:S(2)}, u32[]{:S(2)}) collective-permute-start(bf16[32,2560]{1,0:T(8,128)(2,1)S(1)} %get-tuple-element.38), channel_id=1, source_target_pairs={{0,1},{1,0},{2,3},{3,2},{4,5},{5,4},{6,7},{7,6},{8,9},{9,8},{10,11... | collective-permute-start | bytes 491528 | tf_op jit(solution)/shard_map/ppermute | solution.py:303
  27.9 3.7 %collective-permute-start.11 = (bf16[32,2560]{1,0:T(8,128)(2,1)S(1)}, bf16[32,2560]{1,0:T(8,128)(2,1)S(1)}, u32[]{:S(2)}, u32[]{:S(2)}) collective-permute-start(bf16[32,2560]{1,0:T(8,128)(2,1)S(1)} %get-tuple-element.39), channel_id=1, source_target_pairs={{0,1},{1,0},{2,3},{3,2},{4,5},{5,4},{6,7},{7,6},{8,9},{9,8},{10,11... | collective-permute-start | bytes 491528 | tf_op jit(solution)/shard_map/ppermute | solution.py:303
  28.2 4.9 %collective-permute-start.13 = (bf16[32,2560]{1,0:T(8,128)(2,1)S(1)}, bf16[32,2560]{1,0:T(8,128)(2,1)S(1)}, u32[]{:S(2)}, u32[]{:S(2)}) collective-permute-start(bf16[32,2560]{1,0:T(8,128)(2,1)S(1)} %get-tuple-element.40), channel_id=1, source_target_pairs={{0,1},{1,0},{2,3},{3,2},{4,5},{5,4},{6,7},{7,6},{8,9},{9,8},{10,11... | collective-permute-start | bytes 491528 | tf_op jit(solution)/shard_map/ppermute | solution.py:303
  29.0 9.5 %collective-permute-start.8 = (bf16[32,2688]{1,0:T(8,128)(2,1)S(1)}, bf16[32,2688]{1,0:T(8,128)(2,1)S(1)}, u32[]{:S(2)}, u32[]{:S(2)}) collective-permute-start(bf16[32,2688]{1,0:T(8,128)(2,1)S(1)} %shard_map.98), channel_id=1, source_target_pairs={{8,0},{9,1},{10,2},{11,3},{12,4},{13,5},{14,6},{15,7},{16,8},{17,9... | collective-permute-start | bytes 516104 | tf_op jit(solution)/shard_map/ppermute | solution.py:312
  30.3 12.6 %collective-permute-start.10 = (bf16[32,2688]{1,0:T(8,128)(2,1)S(1)}, bf16[32,2688]{1,0:T(8,128)(2,1)S(1)}, u32[]{:S(2)}, u32[]{:S(2)}) collective-permute-start(bf16[32,2688]{1,0:T(8,128)(2,1)S(1)} %shard_map.99), channel_id=1, source_target_pairs={{8,6},{9,7},{10,0},{11,1},{12,2},{13,3},{14,4},{15,5},{16,14},{17,... | collective-permute-start | bytes 516104 | tf_op jit(solution)/shard_map/ppermute | solution.py:312
  31.7 14.6 %collective-permute-start.12 = (bf16[32,2688]{1,0:T(8,128)(2,1)S(1)}, bf16[32,2688]{1,0:T(8,128)(2,1)S(1)}, u32[]{:S(2)}, u32[]{:S(2)}) collective-permute-start(bf16[32,2688]{1,0:T(8,128)(2,1)S(1)} %shard_map.100), channel_id=1, source_target_pairs={{8,4},{9,5},{10,6},{11,7},{12,0},{13,1},{14,2},{15,3},{16,12},{17,... | collective-permute-start | bytes 516104 | tf_op jit(solution)/shard_map/ppermute | solution.py:312
  33.1 17.1 %collective-permute-start.14 = (bf16[32,2688]{1,0:T(8,128)(2,1)S(1)}, bf16[32,2688]{1,0:T(8,128)(2,1)S(1)}, u32[]{:S(2)}, u32[]{:S(2)}) collective-permute-start(bf16[32,2688]{1,0:T(8,128)(2,1)S(1)} %shard_map.101), channel_id=1, source_target_pairs={{8,2},{9,3},{10,4},{11,5},{12,6},{13,7},{14,0},{15,1},{16,10},{17,... | collective-permute-start | bytes 516104 | tf_op jit(solution)/shard_map/ppermute | solution.py:312

commit v3 on v2

--- a/solution.py
+++ b/solution.py
@@ -33,6 +33,23 @@
 
 def dot(a, b):
     return jnp.dot(a, b, preferred_element_type=F32)
+
+
+def paired(experts):
+    return experts & (experts - 1) == 0
+
+
+def partner(expert, turn, experts):
+    if not paired(experts):
+        return (expert + turn) % experts
+    return expert ^ ((turn - 2) % (experts - 1) + 1 if turn else 0)
+
+
+def turn_to(source, target, experts):
+    if not paired(experts):
+        return lax.rem(target - source + experts, experts)
+    mask = jnp.bitwise_xor(source, target)
+    return jnp.where(mask > 0, lax.rem(mask, experts - 1) + 1, 0)
 
 
 def pack_kernel(experts, main, me, up_in, route_in, slot_in, logit_in, *refs):
@@ -58,7 +75,7 @@
     slope = gate * (1.0 - gate)
     high = slope.astype(BF16).astype(F32)
     number = (iota((1, tokens), 1) + 1).astype(F32)
-    turn = lax.rem(route - me[0] + experts, experts)
+    turn = turn_to(me[0], route, experts)
     place = turn * main + slot
     rows = iota((experts * main, tokens), 0)
     pick = ((rows == place) & (slot < main)).astype(F32).astype(BF16)
@@ -97,7 +114,7 @@
 def arrival_row(natural, me, experts, group, main, total):
     per = main + 1
     source, slot = natural // per, lax.rem(natural, per)
-    turn = lax.rem(me[0] - source // group + experts, experts)
+    turn = turn_to(source // group, me[0], experts)
     lane = lax.rem(lax.rem(source, group) - me[1] + group, group)
     block = lane * experts + turn
     return jnp.where(slot < main, block * main + slot, total * main + block)
@@ -299,15 +316,16 @@
         pairs = []
         for source in range(total):
             e, g = source // group, source % group
-            pairs.append((source, (e + turn) % experts * group + (g - lane) % group))
+            pairs.append((source, partner(e, turn, experts) * group + (g - lane) % group))
         return lax.ppermute(value, "expert", pairs)
 
     def send_back(value, turn):
+        origin = {partner(e, turn, experts): e for e in range(experts)}
         pairs = []
         for section in range(1, sections):
             for source in range(total):
                 e, g = source // group, source % group
-                target = (e - turn) % experts * group + g
+                target = origin[e] * group + g
                 pairs.append((section * total + source, (section - 1) * total + target))
         return lax.ppermute(value, ("section", "expert"), pairs)
 

time: 51.6 us -> 50.7 us (0.983)
  starting transfers between devices: 12.7 us -> 11.4 us
    ppermute x11, starting transfers between devices: 7.54 us -> 6.2 us  [send(): return lax.ppermute(value, 'expert', pairs)]
    ppermute x11, waiting for transfers between devices: 4.08 us -> 5.37 us  [send(): return lax.ppermute(value, 'expert', pairs)]
    ppermute x4, waiting for transfers between devices: 11.7 us -> 10.7 us  [send_back(): return lax.ppermute(value, ('section', 'expert'), pairs)]
  transfers between devices with their start and end apart: 15 -> 15, of which waited for: 9 -> 9; matrix products, arithmetic and copies ran while one was open for 0% -> 0% of each run, Pallas kernels for 16% -> 17%
where the time goes in v3:
time: 50.7 us; the launch traced here: 50.5 us
  Pallas kernels  22.1 us (44%)
  waiting for transfers between devices  16.1 us (32%)
  starting transfers between devices  11.4 us (22%)
  between operations  0.86 us (2%)
    pallas_call x9, Pallas kernels, call(): pl.pallas_call(kernel, out_shape=tuple(outs), cost_estimate=pl.CostEstima...  22.1 us
    ppermute x4, waiting for transfers between devices, send_back(): return lax.ppermute(value, ('section', 'expert'), pairs)  10.7 us
    ppermute x11, starting transfers between devices, send(): return lax.ppermute(value, 'expert', pairs)  6.2 us
    ppermute x11, waiting for transfers between devices, send(): return lax.ppermute(value, 'expert', pairs)  5.37 us
    ppermute x4, starting transfers between devices, send_back(): return lax.ppermute(value, ('section', 'expert'), pairs)  5.17 us
  transfers between devices with their start and end apart: 15, of which 9 were waited for; matrix products, arithmetic and copies ran while one was open for 0% of the time, Pallas kernels for 17%

profile of v3, /device:TPU:0, one launch (start us, length us, event | category | flops | bytes accessed | tf_op | source)
XLA Modules:
  0.0 50.5 jit_solution(16765901052220683164)
XLA Ops:
  0.6 0.1 pad_add_fusion.me
  0.8 0.0 slice-start.4
  0.8 2.2 %shard_map.95 = (bf16[32,2688]{1,0:T(8,128)(2,1)S(1)}, bf16[32,2688]{1,0:T(8,128)(2,1)S(1)}, bf16[32,2688]{1,0:T(8,128)(2,1)S(1)}, bf16[32,2688]{1,0:T(8,128)(2,1)S(1)}) custom-call(s32[2]{0:T(128)S(1)} %pad_add_fusion.me, bf16[128,2560]{1,0:T(8,128)(2,1)} %bitcast.25, s32[1,128]{1,0:T(1,128)} %route_in.1, s32[1,128]{1,0:T(1,128)} %slot_in.1, f32[4,128]{1,0:T(4,128)} %bitcast.26), custom_call_target="tpu_custom_call" | custom-call | flops 20000000000 | bytes 1346568 | tf_op jit(solution)/shard_map/pallas_call | solution.py:283
  3.0 4.0 %collective-permute-start = (bf16[32,2688]{1,0:T(8,128)(2,1)S(1)}, bf16[32,2688]{1,0:T(8,128)(2,1)S(1)}, u32[]{:S(2)}, u32[]{:S(2)}) collective-permute-start(bf16[32,2688]{1,0:T(8,128)(2,1)S(1)} %get-tuple-element.23), channel_id=1, source_target_pairs={{0,6},{1,7},{2,4},{3,5},{4,2},{5,3},{6,0},{7,1},{8,14},{9,15},{10,... | collective-permute-start | bytes 516104 | tf_op jit(solution)/shard_map/ppermute | solution.py:320
  7.0 0.5 %collective-permute-start.1 = (bf16[32,2688]{1,0:T(8,128)(2,1)S(1)}, bf16[32,2688]{1,0:T(8,128)(2,1)S(1)}, u32[]{:S(2)}, u32[]{:S(2)}) collective-permute-start(bf16[32,2688]{1,0:T(8,128)(2,1)S(1)} %get-tuple-element.24), channel_id=1, source_target_pairs={{0,2},{1,3},{2,0},{3,1},{4,6},{5,7},{6,4},{7,5},{8,10},{9,11},{10,... | collective-permute-start | bytes 516104 | tf_op jit(solution)/shard_map/ppermute | solution.py:320
  7.5 0.1 collective-permute-start.2
  7.6 4.2 %shard_map.96 = (bf16[264,2048]{1,0:T(8,128)(2,1)S(1)}, f32[264,2048]{1,0:T(8,128)S(1)}, f32[264,2048]{1,0:T(8,128)S(1)}) custom-call(s32[2]{0:T(128)S(1)} %pad_add_fusion.me, bf16[264,4096]{1,0:T(8,128)(2,1)S(1)} %bitcast.21, bf16[264,4096]{1,0:T(8,128)(2,1)S(1)} %bitcast.22), custom_call_target="tpu_custom_call" | custom-call | flops 2000000000 | bytes 9732104 | tf_op jit(solution)/shard_map/pallas_call | solution.py:283
  11.9 0.3 collective-permute-done.refs_1_.side_ref
  12.2 3.1 %collective-permute-done.1.refs_2_.side_ref = bf16[32,2688]{1,0:T(8,128)(2,1)S(1)} collective-permute-done((bf16[32,2688]{1,0:T(8,128)(2,1)S(1)}, bf16[32,2688]{1,0:T(8,128)(2,1)S(1)}, u32[]{:S(2)}, u32[]{:S(2)}) %collective-permute-start.1) | collective-permute-done | bytes 172064 | tf_op jit(solution)/shard_map/ppermute | solution.py:320
  15.4 0.5 %collective-permute-start.5 = (bf16[32,2688]{1,0:T(8,128)(2,1)S(1)}, bf16[32,2688]{1,0:T(8,128)(2,1)S(1)}, u32[]{:S(2)}, u32[]{:S(2)}) collective-permute-start(bf16[32,2688]{1,0:T(8,128)(2,1)S(1)} %collective-permute-done.1.refs_2_.side_ref), channel_id=1, source_target_pairs={{0,1},{1,0},{2,3},{3,2},{4,5},{5,4},{6,7},{7,6},{8,9},{9,8},{10,11... | collective-permute-start | bytes 516104 | tf_op jit(solution)/shard_map/ppermute | solution.py:320
  15.9 0.0 collective-permute-start.4
  15.9 0.9 %collective-permute-done.6.refs_7_ = bf16[32,2688]{1,0:T(8,128)(2,1)S(1)} collective-permute-done((bf16[32,2688]{1,0:T(8,128)(2,1)S(1)}, bf16[32,2688]{1,0:T(8,128)(2,1)S(1)}, u32[]{:S(2)}, u32[]{:S(2)}) %collective-permute-start.6) | collective-permute-done | bytes 172064 | tf_op jit(solution)/shard_map/ppermute | solution.py:320
  16.8 0.2 collective-permute-done.5.refs_6_
  17.0 0.3 collective-permute-done.4.refs_5_
  17.4 10.0 %shard_map.97 = (bf16[264,4096]{1,0:T(8,128)(2,1)S(1)}, f32[128,2560]{1,0:T(8,128)S(1)}, f32[8,2560]{1,0:T(8,128)S(1)}, bf16[48,2560]{1,0:T(8,128)(2,1)S(1)}, bf...) custom-call(s32[2]{0:T(128)S(1)} %pad_add_fusion.me, ...), custom_call_target="tpu_custom_call" | custom-call | flops 8304721920 | bytes 42553352 | tf_op jit(solution)/shard_map/pallas_call | solution.py:283
  27.4 0.3 collective-permute-start.7
  27.7 0.3 collective-permute-start.9
  27.9 0.2 collective-permute-start.11
  28.2 0.3 collective-permute-start.13
  28.4 0.5 collective-permute-done.7.refs_0_.refs_1_
  29.0 1.3 %collective-permute-start.8 = (bf16[32,2688]{1,0:T(8,128)(2,1)S(1)}, bf16[32,2688]{1,0:T(8,128)(2,1)S(1)}, u32[]{:S(2)}, u32[]{:S(2)}) collective-permute-start(bf16[32,2688]{1,0:T(8,128)(2,1)S(1)} %shard_map.98), channel_id=1, source_target_pairs={{8,0},{9,1},{10,2},{11,3},{12,4},{13,5},{14,6},{15,7},{16,8},{17,9... | collective-permute-start | bytes 516104 | tf_op jit(solution)/shard_map/ppermute | solution.py:330
  30.3 0.1 shard_map.99
  30.4 1.3 %collective-permute-start.10 = (bf16[32,2688]{1,0:T(8,128)(2,1)S(1)}, bf16[32,2688]{1,0:T(8,128)(2,1)S(1)}, u32[]{:S(2)}, u32[]{:S(2)}) collective-permute-start(bf16[32,2688]{1,0:T(8,128)(2,1)S(1)} %shard_map.99), channel_id=1, source_target_pairs={{8,6},{9,7},{10,4},{11,5},{12,2},{13,3},{14,0},{15,1},{16,14},{17,... | collective-permute-start | bytes 516104 | tf_op jit(solution)/shard_map/ppermute | solution.py:330
  31.7 0.1 shard_map.100
  31.7 1.3 %collective-permute-start.12 = (bf16[32,2688]{1,0:T(8,128)(2,1)S(1)}, bf16[32,2688]{1,0:T(8,128)(2,1)S(1)}, u32[]{:S(2)}, u32[]{:S(2)}) collective-permute-start(bf16[32,2688]{1,0:T(8,128)(2,1)S(1)} %shard_map.100), channel_id=1, source_target_pairs={{8,2},{9,3},{10,0},{11,1},{12,6},{13,7},{14,4},{15,5},{16,10},{17,... | collective-permute-start | bytes 516104 | tf_op jit(solution)/shard_map/ppermute | solution.py:330
  33.0 0.1 shard_map.101
  33.1 1.3 %collective-permute-start.14 = (bf16[32,2688]{1,0:T(8,128)(2,1)S(1)}, bf16[32,2688]{1,0:T(8,128)(2,1)S(1)}, u32[]{:S(2)}, u32[]{:S(2)}) collective-permute-start(bf16[32,2688]{1,0:T(8,128)(2,1)S(1)} %shard_map.101), channel_id=1, source_target_pairs={{8,4},{9,5},{10,6},{11,7},{12,0},{13,1},{14,2},{15,3},{16,12},{17,... | collective-permute-start | bytes 516104 | tf_op jit(solution)/shard_map/ppermute | solution.py:330
  34.4 4.2 %shard_map.103 = bf16[264,4096]{1,0:T(8,128)(2,1)} custom-call(s32[2]{0:T(128)S(1)} %pad_add_fusion.me, bf16[264,4096]{1,0:T(8,128)(2,1)S(1)} %get-tuple-element.41.grad_ref), custom_call_target="tpu_custom_call" | custom-call | flops 570949632 | bytes 4325384 | tf_op jit(solution)/shard_map/pallas_call | solution.py:283
  38.6 5.0 %collective-permute-done.10.refs_1_ = bf16[32,2688]{1,0:T(8,128)(2,1)S(1)} collective-permute-done((bf16[32,2688]{1,0:T(8,128)(2,1)S(1)}, bf16[32,2688]{1,0:T(8,128)(2,1)S(1)}, u32[]{:S(2)}, u32[]{:S(2)}) %collective-permute-start.10) | collective-permute-done | bytes 172064 | tf_op jit(solution)/shard_map/ppermute | solution.py:330
  43.6 2.8 %collective-permute-done.12.refs_2_ = bf16[32,2688]{1,0:T(8,128)(2,1)S(1)} collective-permute-done((bf16[32,2688]{1,0:T(8,128)(2,1)S(1)}, bf16[32,2688]{1,0:T(8,128)(2,1)S(1)}, u32[]{:S(2)}, u32[]{:S(2)}) %collective-permute-start.12) | collective-permute-done | bytes 172064 | tf_op jit(solution)/shard_map/ppermute | solution.py:330
  46.4 2.9 %collective-permute-done.14.refs_3_ = bf16[32,2688]{1,0:T(8,128)(2,1)S(1)} collective-permute-done((bf16[32,2688]{1,0:T(8,128)(2,1)S(1)}, bf16[32,2688]{1,0:T(8,128)(2,1)S(1)}, u32[]{:S(2)}, u32[]{:S(2)}) %collective-permute-start.14) | collective-permute-done | bytes 172064 | tf_op jit(solution)/shard_map/ppermute | solution.py:330
  49.3 1.2 %shard_map.102 = bf16[128,2560]{1,0:T(8,128)(2,1)} custom-call(bf16[32,2688]{1,0:T(8,128)(2,1)S(1)} %collective-permute-done.8.refs_0_, bf16[32,2688]{1,0:T(8,128)(2,1)S(1)} %collective-permute-done.10.refs_1_, bf16[32,2688]{1,0:T(8,128)(2,1)S(1)} %collective-permute-done.12.refs_2_, bf16[32,2688]{1,0:T(8,128)(2,1)S(1)} %collective-permute-done.14.refs_3_), custom_call_target="tpu_custom_call" | custom-call | flops 83886080 | bytes 1343488 | tf_op jit(solution)/shard_map/pallas_call | solution.py:283
  (30 shorter events, 0.1 us)
Async XLA Ops:
  0.7 16.6 %slice-start = ((s8[20971520]{0:T(1024)(128)(4,1)}), s8[4194304]{0:T(1024)(128)(4,1)S(1)}, s32[]{:S(2)}) async-start(s8[20971520]{0:T(1024)(128)(4,1)} %bitcast.14), calls=%async_computation | async-start | bytes 8388608
  0.7 16.6 %slice-start.5 = ((s8[10485760]{0:T(1024)(128)(4,1)}), s8[4194304]{0:T(1024)(128)(4,1)S(1)}, s32[]{:S(2)}) async-start(s8[10485760]{0:T(1024)(128)(4,1)} %bitcast.17), calls=%async_computation.5 | async-start | bytes 8388608
  0.7 6.9 %copy-start.1 = (bf16[1,1,264,4096]{3,2,1,0:T(8,128)(2,1)S(1)}, bf16[1,1,264,4096]{3,2,1,0:T(8,128)(2,1)}, u32[]{:S(2)}) copy-start(bf16[1,1,264,4096]{3,2,1,0:T(8,128)(2,1)} %param.12) | copy-start | bytes 6488068
  0.7 16.6 %slice-start.1 = ((s8[20971520]{0:T(1024)(128)(4,1)}), s8[4194304]{0:T(1024)(128)(4,1)S(1)}, s32[]{:S(2)}) async-start(s8[20971520]{0:T(1024)(128)(4,1)} %bitcast.14), calls=%async_computation.1 | async-start | bytes 8388608
  0.7 16.6 %slice-start.2 = ((s8[20971520]{0:T(1024)(128)(4,1)}), s8[4194304]{0:T(1024)(128)(4,1)S(1)}, s32[]{:S(2)}) async-start(s8[20971520]{0:T(1024)(128)(4,1)} %bitcast.14), calls=%async_computation.2 | async-start | bytes 8388608
  0.7 16.6 %slice-start.3 = ((s8[20971520]{0:T(1024)(128)(4,1)}), s8[4194304]{0:T(1024)(128)(4,1)S(1)}, s32[]{:S(2)}) async-start(s8[20971520]{0:T(1024)(128)(4,1)} %bitcast.14), calls=%async_computation.3 | async-start | bytes 8388608
  0.8 16.6 %slice-start.4 = ((s8[20971520]{0:T(1024)(128)(4,1)}), s8[4194304]{0:T(1024)(128)(4,1)S(1)}, s32[]{:S(2)}) async-start(s8[20971520]{0:T(1024)(128)(4,1)} %bitcast.14), calls=%async_computation.4 | async-start | bytes 8388608
  0.8 16.6 %slice-start.6 = ((s8[10485760]{0:T(1024)(128)(4,1)}), s8[4194304]{0:T(1024)(128)(4,1)S(1)}, s32[]{:S(2)}) async-start(s8[10485760]{0:T(1024)(128)(4,1)} %bitcast.17), calls=%async_computation.6 | async-start | bytes 8388608
  0.8 16.6 %slice-start.7 = ((s8[10485760]{0:T(1024)(128)(4,1)}), s8[2097152]{0:T(1024)(128)(4,1)S(1)}, s32[]{:S(2)}) async-start(s8[10485760]{0:T(1024)(128)(4,1)} %bitcast.17), calls=%async_computation.7 | async-start | bytes 4194304
  3.0 9.2 %collective-permute-start = (bf16[32,2688]{1,0:T(8,128)(2,1)S(1)}, bf16[32,2688]{1,0:T(8,128)(2,1)S(1)}, u32[]{:S(2)}, u32[]{:S(2)}) collective-permute-start(bf16[32,2688]{1,0:T(8,128)(2,1)S(1)} %get-tuple-element.23), channel_id=1, source_target_pairs={{0,6},{1,7},{2,4},{3,5},{4,2},{5,3},{6,0},{7,1},{8,14},{9,15},{10,... | collective-permute-start | bytes 516104 | tf_op jit(solution)/shard_map/ppermute | solution.py:320
  7.0 8.4 %collective-permute-start.1 = (bf16[32,2688]{1,0:T(8,128)(2,1)S(1)}, bf16[32,2688]{1,0:T(8,128)(2,1)S(1)}, u32[]{:S(2)}, u32[]{:S(2)}) collective-permute-start(bf16[32,2688]{1,0:T(8,128)(2,1)S(1)} %get-tuple-element.24), channel_id=1, source_target_pairs={{0,2},{1,3},{2,0},{3,1},{4,6},{5,7},{6,4},{7,5},{8,10},{9,11},{10,... | collective-permute-start | bytes 516104 | tf_op jit(solution)/shard_map/ppermute | solution.py:320
  7.5 7.8 %collective-permute-start.2 = (bf16[32,2688]{1,0:T(8,128)(2,1)S(1)}, bf16[32,2688]{1,0:T(8,128)(2,1)S(1)}, u32[]{:S(2)}, u32[]{:S(2)}) collective-permute-start(bf16[32,2688]{1,0:T(8,128)(2,1)S(1)} %get-tuple-element.25), channel_id=1, source_target_pairs={{0,4},{1,5},{2,6},{3,7},{4,0},{5,1},{6,2},{7,3},{8,12},{9,13},{10,... | collective-permute-start | bytes 516104 | tf_op jit(solution)/shard_map/ppermute | solution.py:320
  7.6 8.2 %collective-permute-start.3 = (bf16[32,2688]{1,0:T(8,128)(2,1)S(1)}, bf16[32,2688]{1,0:T(8,128)(2,1)S(1)}, u32[]{:S(2)}, u32[]{:S(2)}) collective-permute-start(bf16[32,2688]{1,0:T(8,128)(2,1)S(1)} %get-tuple-element.22.refs_0_.side_ref), channel_id=1, source_target_pairs={{0,1},{1,0},{2,3},{3,2},{4,5},{5,4},{6,7},{7,6},{8,9},{9,8},{10,11... | collective-permute-start | bytes 516104 | tf_op jit(solution)/shard_map/ppermute | solution.py:320
  7.6 9.7 %copy-start = (bf16[1,2560,4]{1,2,0:T(4,128)(2,1)S(1)}, bf16[1,2560,4]{1,2,0:T(4,128)(2,1)}, u32[]{:S(2)}) copy-start(bf16[1,2560,4]{1,2,0:T(4,128)(2,1)} %param.15) | copy-start | bytes 61444
  15.4 1.4 %collective-permute-start.6 = (bf16[32,2688]{1,0:T(8,128)(2,1)S(1)}, bf16[32,2688]{1,0:T(8,128)(2,1)S(1)}, u32[]{:S(2)}, u32[]{:S(2)}) collective-permute-start(bf16[32,2688]{1,0:T(8,128)(2,1)S(1)} %collective-permute-done.2.refs_3_.side_ref), channel_id=1, source_target_pairs={{0,1},{1,0},{2,3},{3,2},{4,5},{5,4},{6,7},{7,6},{8,9},{9,8},{10,11... | collective-permute-start | bytes 516104 | tf_op jit(solution)/shard_map/ppermute | solution.py:320
  15.4 1.7 %collective-permute-start.5 = (bf16[32,2688]{1,0:T(8,128)(2,1)S(1)}, bf16[32,2688]{1,0:T(8,128)(2,1)S(1)}, u32[]{:S(2)}, u32[]{:S(2)}) collective-permute-start(bf16[32,2688]{1,0:T(8,128)(2,1)S(1)} %collective-permute-done.1.refs_2_.side_ref), channel_id=1, source_target_pairs={{0,1},{1,0},{2,3},{3,2},{4,5},{5,4},{6,7},{7,6},{8,9},{9,8},{10,11... | collective-permute-start | bytes 516104 | tf_op jit(solution)/shard_map/ppermute | solution.py:320
  15.9 1.4 %collective-permute-start.4 = (bf16[32,2688]{1,0:T(8,128)(2,1)S(1)}, bf16[32,2688]{1,0:T(8,128)(2,1)S(1)}, u32[]{:S(2)}, u32[]{:S(2)}) collective-permute-start(bf16[32,2688]{1,0:T(8,128)(2,1)S(1)} %collective-permute-done.refs_1_.side_ref), channel_id=1, source_target_pairs={{0,1},{1,0},{2,3},{3,2},{4,5},{5,4},{6,7},{7,6},{8,9},{9,8},{10,11... | collective-permute-start | bytes 516104 | tf_op jit(solution)/shard_map/ppermute | solution.py:320
  27.4 1.6 %collective-permute-start.7 = (bf16[48,2560]{1,0:T(8,128)(2,1)S(1)}, bf16[48,2560]{1,0:T(8,128)(2,1)S(1)}, u32[]{:S(2)}, u32[]{:S(2)}) collective-permute-start(bf16[48,2560]{1,0:T(8,128)(2,1)S(1)} %get-tuple-element.37), channel_id=1, source_target_pairs={{0,1},{1,0},{2,3},{3,2},{4,5},{5,4},{6,7},{7,6},{8,9},{9,8},{10,11... | collective-permute-start | bytes 737288 | tf_op jit(solution)/shard_map/ppermute | solution.py:320
  27.7 2.6 %collective-permute-start.9 = (bf16[32,2560]{1,0:T(8,128)(2,1)S(1)}, bf16[32,2560]{1,0:T(8,128)(2,1)S(1)}, u32[]{:S(2)}, u32[]{:S(2)}) collective-permute-start(bf16[32,2560]{1,0:T(8,128)(2,1)S(1)} %get-tuple-element.38), channel_id=1, source_target_pairs={{0,1},{1,0},{2,3},{3,2},{4,5},{5,4},{6,7},{7,6},{8,9},{9,8},{10,11... | collective-permute-start | bytes 491528 | tf_op jit(solution)/shard_map/ppermute | solution.py:320
  27.9 3.7 %collective-permute-start.11 = (bf16[32,2560]{1,0:T(8,128)(2,1)S(1)}, bf16[32,2560]{1,0:T(8,128)(2,1)S(1)}, u32[]{:S(2)}, u32[]{:S(2)}) collective-permute-start(bf16[32,2560]{1,0:T(8,128)(2,1)S(1)} %get-tuple-element.39), channel_id=1, source_target_pairs={{0,1},{1,0},{2,3},{3,2},{4,5},{5,4},{6,7},{7,6},{8,9},{9,8},{10,11... | collective-permute-start | bytes 491528 | tf_op jit(solution)/shard_map/ppermute | solution.py:320
  28.2 4.9 %collective-permute-start.13 = (bf16[32,2560]{1,0:T(8,128)(2,1)S(1)}, bf16[32,2560]{1,0:T(8,128)(2,1)S(1)}, u32[]{:S(2)}, u32[]{:S(2)}) collective-permute-start(bf16[32,2560]{1,0:T(8,128)(2,1)S(1)} %get-tuple-element.40), channel_id=1, source_target_pairs={{0,1},{1,0},{2,3},{3,2},{4,5},{5,4},{6,7},{7,6},{8,9},{9,8},{10,11... | collective-permute-start | bytes 491528 | tf_op jit(solution)/shard_map/ppermute | solution.py:320
  29.0 9.6 %collective-permute-start.8 = (bf16[32,2688]{1,0:T(8,128)(2,1)S(1)}, bf16[32,2688]{1,0:T(8,128)(2,1)S(1)}, u32[]{:S(2)}, u32[]{:S(2)}) collective-permute-start(bf16[32,2688]{1,0:T(8,128)(2,1)S(1)} %shard_map.98), channel_id=1, source_target_pairs={{8,0},{9,1},{10,2},{11,3},{12,4},{13,5},{14,6},{15,7},{16,8},{17,9... | collective-permute-start | bytes 516104 | tf_op jit(solution)/shard_map/ppermute | solution.py:330
  30.4 13.2 %collective-permute-start.10 = (bf16[32,2688]{1,0:T(8,128)(2,1)S(1)}, bf16[32,2688]{1,0:T(8,128)(2,1)S(1)}, u32[]{:S(2)}, u32[]{:S(2)}) collective-permute-start(bf16[32,2688]{1,0:T(8,128)(2,1)S(1)} %shard_map.99), channel_id=1, source_target_pairs={{8,6},{9,7},{10,4},{11,5},{12,2},{13,3},{14,0},{15,1},{16,14},{17,... | collective-permute-start | bytes 516104 | tf_op jit(solution)/shard_map/ppermute | solution.py:330
  31.7 14.7 %collective-permute-start.12 = (bf16[32,2688]{1,0:T(8,128)(2,1)S(1)}, bf16[32,2688]{1,0:T(8,128)(2,1)S(1)}, u32[]{:S(2)}, u32[]{:S(2)}) collective-permute-start(bf16[32,2688]{1,0:T(8,128)(2,1)S(1)} %shard_map.100), channel_id=1, source_target_pairs={{8,2},{9,3},{10,0},{11,1},{12,6},{13,7},{14,4},{15,5},{16,10},{17,... | collective-permute-start | bytes 516104 | tf_op jit(solution)/shard_map/ppermute | solution.py:330
  33.1 16.2 %collective-permute-start.14 = (bf16[32,2688]{1,0:T(8,128)(2,1)S(1)}, bf16[32,2688]{1,0:T(8,128)(2,1)S(1)}, u32[]{:S(2)}, u32[]{:S(2)}) collective-permute-start(bf16[32,2688]{1,0:T(8,128)(2,1)S(1)} %shard_map.101), channel_id=1, source_target_pairs={{8,4},{9,5},{10,6},{11,7},{12,0},{13,1},{14,2},{15,3},{16,12},{17,... | collective-permute-start | bytes 516104 | tf_op jit(solution)/shard_map/ppermute | solution.py:330

commit v4 on v3

--- a/solution.py
+++ b/solution.py
@@ -42,14 +42,13 @@
 def partner(expert, turn, experts):
     if not paired(experts):
         return (expert + turn) % experts
-    return expert ^ ((turn - 2) % (experts - 1) + 1 if turn else 0)
+    return expert ^ turn
 
 
 def turn_to(source, target, experts):
     if not paired(experts):
         return lax.rem(target - source + experts, experts)
-    mask = jnp.bitwise_xor(source, target)
-    return jnp.where(mask > 0, lax.rem(mask, experts - 1) + 1, 0)
+    return jnp.bitwise_xor(source, target)
 
 
 def pack_kernel(experts, main, me, up_in, route_in, slot_in, logit_in, *refs):
@@ -390,12 +389,11 @@
         out_specs=[VMEM] * (3 + (group - 1) * experts),
         scratch_shapes=scratch,
     )
-    others = [
-        [send(sent[(lane - 1) * experts + k], 0, -lane) for lane in range(1, group)]
-        for k in range(experts)
-    ]
-    returned = []
-    for k in range(experts):
+    others, returned = {}, {}
+    back = [0, experts - 1, *range(1, experts - 1)]
+    for k in back:
+        others[k] = [send(sent[(lane - 1) * experts + k], 0, -lane) for lane in range(1, group)]
+    for k in back:
         (merged,) = call(
             functools.partial(merge_kernel, experts, group, main, k),
             [block],
@@ -404,7 +402,8 @@
             in_specs=[VMEM] * (1 + 2 * group),
             out_specs=[VMEM],
         )
-        returned.append(send_back(merged, k))
+        returned[k] = send_back(merged, k)
+    returned = [returned[k] for k in range(experts)]
 
     columns = min(1024, 2 * half)
     (hidden_grads,) = call(

time: 50.7 us -> 51 us (level)
  waiting for transfers between devices: 16.1 us -> 16.7 us
  transfers between devices with their start and end apart: 15 -> 15, of which waited for: 9 -> 8; matrix products, arithmetic and copies ran while one was open for 0% -> 0% of each run, Pallas kernels for 17% -> 16%
where the time goes in v4:
time: 51 us; the launch traced here: 50.8 us
  Pallas kernels  21.8 us (43%)
  waiting for transfers between devices  16.7 us (33%)
  starting transfers between devices  11.3 us (22%)
  between operations  0.87 us (2%)
    pallas_call x9, Pallas kernels, call(): pl.pallas_call(kernel, out_shape=tuple(outs), cost_estimate=pl.CostEstima...  21.8 us
    ppermute x4, waiting for transfers between devices, send_back(): return lax.ppermute(value, ('section', 'expert'), pairs)  11 us
    ppermute x11, starting transfers between devices, send(): return lax.ppermute(value, 'expert', pairs)  6.15 us
    ppermute x11, waiting for transfers between devices, send(): return lax.ppermute(value, 'expert', pairs)  5.73 us
    ppermute x4, starting transfers between devices, send_back(): return lax.ppermute(value, ('section', 'expert'), pairs)  5.17 us
  transfers between devices with their start and end apart: 15, of which 8 were waited for; matrix products, arithmetic and copies ran while one was open for 0% of the time, Pallas kernels for 16%

profile of v4, /device:TPU:0, one launch (start us, length us, event | category | flops | bytes accessed | tf_op | source)
XLA Modules:
  0.0 50.8 jit_solution(8452527388737330477)
XLA Ops:
  0.6 0.1 pad_add_fusion.me
  0.7 0.0 slice-start.3
  0.8 0.0 slice-start.4
  0.8 2.2 %shard_map.95 = (bf16[32,2688]{1,0:T(8,128)(2,1)S(1)}, bf16[32,2688]{1,0:T(8,128)(2,1)S(1)}, bf16[32,2688]{1,0:T(8,128)(2,1)S(1)}, bf16[32,2688]{1,0:T(8,128)(2,1)S(1)}) custom-call(s32[2]{0:T(128)S(1)} %pad_add_fusion.me, bf16[128,2560]{1,0:T(8,128)(2,1)} %bitcast.25, s32[1,128]{1,0:T(1,128)} %route_in.1, s32[1,128]{1,0:T(1,128)} %slot_in.1, f32[4,128]{1,0:T(4,128)} %bitcast.26), custom_call_target="tpu_custom_call" | custom-call | flops 20000000000 | bytes 1346568 | tf_op jit(solution)/shard_map/pallas_call | solution.py:282
  3.0 3.0 %collective-permute-start = (bf16[32,2688]{1,0:T(8,128)(2,1)S(1)}, bf16[32,2688]{1,0:T(8,128)(2,1)S(1)}, u32[]{:S(2)}, u32[]{:S(2)}) collective-permute-start(bf16[32,2688]{1,0:T(8,128)(2,1)S(1)} %get-tuple-element.23), channel_id=1, source_target_pairs={{0,2},{1,3},{2,0},{3,1},{4,6},{5,7},{6,4},{7,5},{8,10},{9,11},{10,... | collective-permute-start | bytes 516104 | tf_op jit(solution)/shard_map/ppermute | solution.py:319
  6.0 1.5 %collective-permute-start.1 = (bf16[32,2688]{1,0:T(8,128)(2,1)S(1)}, bf16[32,2688]{1,0:T(8,128)(2,1)S(1)}, u32[]{:S(2)}, u32[]{:S(2)}) collective-permute-start(bf16[32,2688]{1,0:T(8,128)(2,1)S(1)} %get-tuple-element.24), channel_id=1, source_target_pairs={{0,4},{1,5},{2,6},{3,7},{4,0},{5,1},{6,2},{7,3},{8,12},{9,13},{10,... | collective-permute-start | bytes 516104 | tf_op jit(solution)/shard_map/ppermute | solution.py:319
  7.6 0.0 collective-permute-start.2
  7.6 4.1 %shard_map.96 = (bf16[264,2048]{1,0:T(8,128)(2,1)S(1)}, f32[264,2048]{1,0:T(8,128)S(1)}, f32[264,2048]{1,0:T(8,128)S(1)}) custom-call(s32[2]{0:T(128)S(1)} %pad_add_fusion.me, bf16[264,4096]{1,0:T(8,128)(2,1)S(1)} %bitcast.21, bf16[264,4096]{1,0:T(8,128)(2,1)S(1)} %bitcast.22), custom_call_target="tpu_custom_call" | custom-call | flops 2000000000 | bytes 9732104 | tf_op jit(solution)/shard_map/pallas_call | solution.py:282
  11.7 3.8 %collective-permute-done.1.refs_2_.side_ref = bf16[32,2688]{1,0:T(8,128)(2,1)S(1)} collective-permute-done((bf16[32,2688]{1,0:T(8,128)(2,1)S(1)}, bf16[32,2688]{1,0:T(8,128)(2,1)S(1)}, u32[]{:S(2)}, u32[]{:S(2)}) %collective-permute-start.1) | collective-permute-done | bytes 172064 | tf_op jit(solution)/shard_map/ppermute | solution.py:319
  15.6 0.5 collective-permute-start.5
  16.1 0.0 collective-permute-start.4
  16.1 0.9 %collective-permute-done.6.refs_7_ = bf16[32,2688]{1,0:T(8,128)(2,1)S(1)} collective-permute-done((bf16[32,2688]{1,0:T(8,128)(2,1)S(1)}, bf16[32,2688]{1,0:T(8,128)(2,1)S(1)}, u32[]{:S(2)}, u32[]{:S(2)}) %collective-permute-start.6) | collective-permute-done | bytes 172064 | tf_op jit(solution)/shard_map/ppermute | solution.py:319
  17.0 0.2 collective-permute-done.5.refs_6_
  17.2 0.3 collective-permute-done.4.refs_5_
  17.6 10.0 %shard_map.97 = (bf16[264,4096]{1,0:T(8,128)(2,1)S(1)}, f32[128,2560]{1,0:T(8,128)S(1)}, f32[8,2560]{1,0:T(8,128)S(1)}, bf16[48,2560]{1,0:T(8,128)(2,1)S(1)}, bf...) custom-call(s32[2]{0:T(128)S(1)} %pad_add_fusion.me, ...), custom_call_target="tpu_custom_call" | custom-call | flops 8304721920 | bytes 42553352 | tf_op jit(solution)/shard_map/pallas_call | solution.py:282
  27.6 0.3 collective-permute-start.7
  27.9 0.3 collective-permute-start.9
  28.1 0.2 collective-permute-start.11
  28.4 0.3 collective-permute-start.13
  28.6 0.5 collective-permute-done.7.refs_0_.refs_1_
  29.2 1.3 %collective-permute-start.8 = (bf16[32,2688]{1,0:T(8,128)(2,1)S(1)}, bf16[32,2688]{1,0:T(8,128)(2,1)S(1)}, u32[]{:S(2)}, u32[]{:S(2)}) collective-permute-start(bf16[32,2688]{1,0:T(8,128)(2,1)S(1)} %shard_map.98), channel_id=1, source_target_pairs={{8,0},{9,1},{10,2},{11,3},{12,4},{13,5},{14,6},{15,7},{16,8},{17,9... | collective-permute-start | bytes 516104 | tf_op jit(solution)/shard_map/ppermute | solution.py:329
  30.5 0.1 shard_map.99
  30.6 1.3 %collective-permute-start.10 = (bf16[32,2688]{1,0:T(8,128)(2,1)S(1)}, bf16[32,2688]{1,0:T(8,128)(2,1)S(1)}, u32[]{:S(2)}, u32[]{:S(2)}) collective-permute-start(bf16[32,2688]{1,0:T(8,128)(2,1)S(1)} %shard_map.99), channel_id=1, source_target_pairs={{8,2},{9,3},{10,0},{11,1},{12,6},{13,7},{14,4},{15,5},{16,10},{17,... | collective-permute-start | bytes 516104 | tf_op jit(solution)/shard_map/ppermute | solution.py:329
  31.9 0.1 shard_map.100
  31.9 1.3 %collective-permute-start.12 = (bf16[32,2688]{1,0:T(8,128)(2,1)S(1)}, bf16[32,2688]{1,0:T(8,128)(2,1)S(1)}, u32[]{:S(2)}, u32[]{:S(2)}) collective-permute-start(bf16[32,2688]{1,0:T(8,128)(2,1)S(1)} %shard_map.100), channel_id=1, source_target_pairs={{8,4},{9,5},{10,6},{11,7},{12,0},{13,1},{14,2},{15,3},{16,12},{17,... | collective-permute-start | bytes 516104 | tf_op jit(solution)/shard_map/ppermute | solution.py:329
  33.2 0.1 shard_map.101
  33.3 1.3 %collective-permute-start.14 = (bf16[32,2688]{1,0:T(8,128)(2,1)S(1)}, bf16[32,2688]{1,0:T(8,128)(2,1)S(1)}, u32[]{:S(2)}, u32[]{:S(2)}) collective-permute-start(bf16[32,2688]{1,0:T(8,128)(2,1)S(1)} %shard_map.101), channel_id=1, source_target_pairs={{8,6},{9,7},{10,4},{11,5},{12,2},{13,3},{14,0},{15,1},{16,14},{17,... | collective-permute-start | bytes 516104 | tf_op jit(solution)/shard_map/ppermute | solution.py:329
  34.6 4.0 %shard_map.103 = bf16[264,4096]{1,0:T(8,128)(2,1)} custom-call(s32[2]{0:T(128)S(1)} %pad_add_fusion.me, bf16[264,4096]{1,0:T(8,128)(2,1)S(1)} %get-tuple-element.41.grad_ref), custom_call_target="tpu_custom_call" | custom-call | flops 570949632 | bytes 4325384 | tf_op jit(solution)/shard_map/pallas_call | solution.py:282
  38.6 4.0 %collective-permute-done.10.refs_1_ = bf16[32,2688]{1,0:T(8,128)(2,1)S(1)} collective-permute-done((bf16[32,2688]{1,0:T(8,128)(2,1)S(1)}, bf16[32,2688]{1,0:T(8,128)(2,1)S(1)}, u32[]{:S(2)}, u32[]{:S(2)}) %collective-permute-start.10) | collective-permute-done | bytes 172064 | tf_op jit(solution)/shard_map/ppermute | solution.py:329
  42.7 4.0 %collective-permute-done.12.refs_2_ = bf16[32,2688]{1,0:T(8,128)(2,1)S(1)} collective-permute-done((bf16[32,2688]{1,0:T(8,128)(2,1)S(1)}, bf16[32,2688]{1,0:T(8,128)(2,1)S(1)}, u32[]{:S(2)}, u32[]{:S(2)}) %collective-permute-start.12) | collective-permute-done | bytes 172064 | tf_op jit(solution)/shard_map/ppermute | solution.py:329
  46.7 3.0 %collective-permute-done.14.refs_3_ = bf16[32,2688]{1,0:T(8,128)(2,1)S(1)} collective-permute-done((bf16[32,2688]{1,0:T(8,128)(2,1)S(1)}, bf16[32,2688]{1,0:T(8,128)(2,1)S(1)}, u32[]{:S(2)}, u32[]{:S(2)}) %collective-permute-start.14) | collective-permute-done | bytes 172064 | tf_op jit(solution)/shard_map/ppermute | solution.py:329
  49.6 1.2 %shard_map.102 = bf16[128,2560]{1,0:T(8,128)(2,1)} custom-call(bf16[32,2688]{1,0:T(8,128)(2,1)S(1)} %collective-permute-done.8.refs_0_, bf16[32,2688]{1,0:T(8,128)(2,1)S(1)} %collective-permute-done.10.refs_1_, bf16[32,2688]{1,0:T(8,128)(2,1)S(1)} %collective-permute-done.12.refs_2_, bf16[32,2688]{1,0:T(8,128)(2,1)S(1)} %collective-permute-done.14.refs_3_), custom_call_target="tpu_custom_call" | custom-call | flops 83886080 | bytes 1343488 | tf_op jit(solution)/shard_map/pallas_call | solution.py:282
  (30 shorter events, 0.1 us)
Async XLA Ops:
  0.7 16.8 %slice-start = ((s8[20971520]{0:T(1024)(128)(4,1)}), s8[4194304]{0:T(1024)(128)(4,1)S(1)}, s32[]{:S(2)}) async-start(s8[20971520]{0:T(1024)(128)(4,1)} %bitcast.14), calls=%async_computation | async-start | bytes 8388608
  0.7 16.8 %slice-start.5 = ((s8[10485760]{0:T(1024)(128)(4,1)}), s8[4194304]{0:T(1024)(128)(4,1)S(1)}, s32[]{:S(2)}) async-start(s8[10485760]{0:T(1024)(128)(4,1)} %bitcast.17), calls=%async_computation.5 | async-start | bytes 8388608
  0.7 6.9 %copy-start.1 = (bf16[1,1,264,4096]{3,2,1,0:T(8,128)(2,1)S(1)}, bf16[1,1,264,4096]{3,2,1,0:T(8,128)(2,1)}, u32[]{:S(2)}) copy-start(bf16[1,1,264,4096]{3,2,1,0:T(8,128)(2,1)} %param.12) | copy-start | bytes 6488068
  0.7 16.8 %slice-start.1 = ((s8[20971520]{0:T(1024)(128)(4,1)}), s8[4194304]{0:T(1024)(128)(4,1)S(1)}, s32[]{:S(2)}) async-start(s8[20971520]{0:T(1024)(128)(4,1)} %bitcast.14), calls=%async_computation.1 | async-start | bytes 8388608
  0.7 16.8 %slice-start.2 = ((s8[20971520]{0:T(1024)(128)(4,1)}), s8[4194304]{0:T(1024)(128)(4,1)S(1)}, s32[]{:S(2)}) async-start(s8[20971520]{0:T(1024)(128)(4,1)} %bitcast.14), calls=%async_computation.2 | async-start | bytes 8388608
  0.7 16.8 %slice-start.3 = ((s8[20971520]{0:T(1024)(128)(4,1)}), s8[4194304]{0:T(1024)(128)(4,1)S(1)}, s32[]{:S(2)}) async-start(s8[20971520]{0:T(1024)(128)(4,1)} %bitcast.14), calls=%async_computation.3 | async-start | bytes 8388608
  0.8 16.8 %slice-start.4 = ((s8[20971520]{0:T(1024)(128)(4,1)}), s8[4194304]{0:T(1024)(128)(4,1)S(1)}, s32[]{:S(2)}) async-start(s8[20971520]{0:T(1024)(128)(4,1)} %bitcast.14), calls=%async_computation.4 | async-start | bytes 8388608
  0.8 16.8 %slice-start.6 = ((s8[10485760]{0:T(1024)(128)(4,1)}), s8[4194304]{0:T(1024)(128)(4,1)S(1)}, s32[]{:S(2)}) async-start(s8[10485760]{0:T(1024)(128)(4,1)} %bitcast.17), calls=%async_computation.6 | async-start | bytes 8388608
  0.8 16.8 %slice-start.7 = ((s8[10485760]{0:T(1024)(128)(4,1)}), s8[2097152]{0:T(1024)(128)(4,1)S(1)}, s32[]{:S(2)}) async-start(s8[10485760]{0:T(1024)(128)(4,1)} %bitcast.17), calls=%async_computation.7 | async-start | bytes 4194304
  3.0 8.7 %collective-permute-start = (bf16[32,2688]{1,0:T(8,128)(2,1)S(1)}, bf16[32,2688]{1,0:T(8,128)(2,1)S(1)}, u32[]{:S(2)}, u32[]{:S(2)}) collective-permute-start(bf16[32,2688]{1,0:T(8,128)(2,1)S(1)} %get-tuple-element.23), channel_id=1, source_target_pairs={{0,2},{1,3},{2,0},{3,1},{4,6},{5,7},{6,4},{7,5},{8,10},{9,11},{10,... | collective-permute-start | bytes 516104 | tf_op jit(solution)/shard_map/ppermute | solution.py:319
  6.0 9.5 %collective-permute-start.1 = (bf16[32,2688]{1,0:T(8,128)(2,1)S(1)}, bf16[32,2688]{1,0:T(8,128)(2,1)S(1)}, u32[]{:S(2)}, u32[]{:S(2)}) collective-permute-start(bf16[32,2688]{1,0:T(8,128)(2,1)S(1)} %get-tuple-element.24), channel_id=1, source_target_pairs={{0,4},{1,5},{2,6},{3,7},{4,0},{5,1},{6,2},{7,3},{8,12},{9,13},{10,... | collective-permute-start | bytes 516104 | tf_op jit(solution)/shard_map/ppermute | solution.py:319
  7.6 8.0 %collective-permute-start.2 = (bf16[32,2688]{1,0:T(8,128)(2,1)S(1)}, bf16[32,2688]{1,0:T(8,128)(2,1)S(1)}, u32[]{:S(2)}, u32[]{:S(2)}) collective-permute-start(bf16[32,2688]{1,0:T(8,128)(2,1)S(1)} %get-tuple-element.25), channel_id=1, source_target_pairs={{0,6},{1,7},{2,4},{3,5},{4,2},{5,3},{6,0},{7,1},{8,14},{9,15},{10,... | collective-permute-start | bytes 516104 | tf_op jit(solution)/shard_map/ppermute | solution.py:319
  7.6 8.5 %collective-permute-start.3 = (bf16[32,2688]{1,0:T(8,128)(2,1)S(1)}, bf16[32,2688]{1,0:T(8,128)(2,1)S(1)}, u32[]{:S(2)}, u32[]{:S(2)}) collective-permute-start(bf16[32,2688]{1,0:T(8,128)(2,1)S(1)} %get-tuple-element.22.refs_0_.side_ref), channel_id=1, source_target_pairs={{0,1},{1,0},{2,3},{3,2},{4,5},{5,4},{6,7},{7,6},{8,9},{9,8},{10,11... | collective-permute-start | bytes 516104 | tf_op jit(solution)/shard_map/ppermute | solution.py:319
  7.6 10.0 %copy-start = (bf16[1,2560,4]{1,2,0:T(4,128)(2,1)S(1)}, bf16[1,2560,4]{1,2,0:T(4,128)(2,1)}, u32[]{:S(2)}) copy-start(bf16[1,2560,4]{1,2,0:T(4,128)(2,1)} %param.15) | copy-start | bytes 61444
  15.6 1.4 %collective-permute-start.6 = (bf16[32,2688]{1,0:T(8,128)(2,1)S(1)}, bf16[32,2688]{1,0:T(8,128)(2,1)S(1)}, u32[]{:S(2)}, u32[]{:S(2)}) collective-permute-start(bf16[32,2688]{1,0:T(8,128)(2,1)S(1)} %collective-permute-done.2.refs_3_.side_ref), channel_id=1, source_target_pairs={{0,1},{1,0},{2,3},{3,2},{4,5},{5,4},{6,7},{7,6},{8,9},{9,8},{10,11... | collective-permute-start | bytes 516104 | tf_op jit(solution)/shard_map/ppermute | solution.py:319
  15.6 1.7 %collective-permute-start.5 = (bf16[32,2688]{1,0:T(8,128)(2,1)S(1)}, bf16[32,2688]{1,0:T(8,128)(2,1)S(1)}, u32[]{:S(2)}, u32[]{:S(2)}) collective-permute-start(bf16[32,2688]{1,0:T(8,128)(2,1)S(1)} %collective-permute-done.1.refs_2_.side_ref), channel_id=1, source_target_pairs={{0,1},{1,0},{2,3},{3,2},{4,5},{5,4},{6,7},{7,6},{8,9},{9,8},{10,11... | collective-permute-start | bytes 516104 | tf_op jit(solution)/shard_map/ppermute | solution.py:319
  16.1 1.4 %collective-permute-start.4 = (bf16[32,2688]{1,0:T(8,128)(2,1)S(1)}, bf16[32,2688]{1,0:T(8,128)(2,1)S(1)}, u32[]{:S(2)}, u32[]{:S(2)}) collective-permute-start(bf16[32,2688]{1,0:T(8,128)(2,1)S(1)} %collective-permute-done.refs_1_.side_ref), channel_id=1, source_target_pairs={{0,1},{1,0},{2,3},{3,2},{4,5},{5,4},{6,7},{7,6},{8,9},{9,8},{10,11... | collective-permute-start | bytes 516104 | tf_op jit(solution)/shard_map/ppermute | solution.py:319
  27.6 1.6 %collective-permute-start.7 = (bf16[48,2560]{1,0:T(8,128)(2,1)S(1)}, bf16[48,2560]{1,0:T(8,128)(2,1)S(1)}, u32[]{:S(2)}, u32[]{:S(2)}) collective-permute-start(bf16[48,2560]{1,0:T(8,128)(2,1)S(1)} %get-tuple-element.37), channel_id=1, source_target_pairs={{0,1},{1,0},{2,3},{3,2},{4,5},{5,4},{6,7},{7,6},{8,9},{9,8},{10,11... | collective-permute-start | bytes 737288 | tf_op jit(solution)/shard_map/ppermute | solution.py:319
  27.9 2.6 %collective-permute-start.9 = (bf16[32,2560]{1,0:T(8,128)(2,1)S(1)}, bf16[32,2560]{1,0:T(8,128)(2,1)S(1)}, u32[]{:S(2)}, u32[]{:S(2)}) collective-permute-start(bf16[32,2560]{1,0:T(8,128)(2,1)S(1)} %get-tuple-element.38), channel_id=1, source_target_pairs={{0,1},{1,0},{2,3},{3,2},{4,5},{5,4},{6,7},{7,6},{8,9},{9,8},{10,11... | collective-permute-start | bytes 491528 | tf_op jit(solution)/shard_map/ppermute | solution.py:319
  28.1 3.7 %collective-permute-start.11 = (bf16[32,2560]{1,0:T(8,128)(2,1)S(1)}, bf16[32,2560]{1,0:T(8,128)(2,1)S(1)}, u32[]{:S(2)}, u32[]{:S(2)}) collective-permute-start(bf16[32,2560]{1,0:T(8,128)(2,1)S(1)} %get-tuple-element.39), channel_id=1, source_target_pairs={{0,1},{1,0},{2,3},{3,2},{4,5},{5,4},{6,7},{7,6},{8,9},{9,8},{10,11... | collective-permute-start | bytes 491528 | tf_op jit(solution)/shard_map/ppermute | solution.py:319
  28.4 4.9 %collective-permute-start.13 = (bf16[32,2560]{1,0:T(8,128)(2,1)S(1)}, bf16[32,2560]{1,0:T(8,128)(2,1)S(1)}, u32[]{:S(2)}, u32[]{:S(2)}) collective-permute-start(bf16[32,2560]{1,0:T(8,128)(2,1)S(1)} %get-tuple-element.40), channel_id=1, source_target_pairs={{0,1},{1,0},{2,3},{3,2},{4,5},{5,4},{6,7},{7,6},{8,9},{9,8},{10,11... | collective-permute-start | bytes 491528 | tf_op jit(solution)/shard_map/ppermute | solution.py:319
  29.2 9.4 %collective-permute-start.8 = (bf16[32,2688]{1,0:T(8,128)(2,1)S(1)}, bf16[32,2688]{1,0:T(8,128)(2,1)S(1)}, u32[]{:S(2)}, u32[]{:S(2)}) collective-permute-start(bf16[32,2688]{1,0:T(8,128)(2,1)S(1)} %shard_map.98), channel_id=1, source_target_pairs={{8,0},{9,1},{10,2},{11,3},{12,4},{13,5},{14,6},{15,7},{16,8},{17,9... | collective-permute-start | bytes 516104 | tf_op jit(solution)/shard_map/ppermute | solution.py:329
  30.6 12.1 %collective-permute-start.10 = (bf16[32,2688]{1,0:T(8,128)(2,1)S(1)}, bf16[32,2688]{1,0:T(8,128)(2,1)S(1)}, u32[]{:S(2)}, u32[]{:S(2)}) collective-permute-start(bf16[32,2688]{1,0:T(8,128)(2,1)S(1)} %shard_map.99), channel_id=1, source_target_pairs={{8,2},{9,3},{10,0},{11,1},{12,6},{13,7},{14,4},{15,5},{16,10},{17,... | collective-permute-start | bytes 516104 | tf_op jit(solution)/shard_map/ppermute | solution.py:329
  31.9 14.7 %collective-permute-start.12 = (bf16[32,2688]{1,0:T(8,128)(2,1)S(1)}, bf16[32,2688]{1,0:T(8,128)(2,1)S(1)}, u32[]{:S(2)}, u32[]{:S(2)}) collective-permute-start(bf16[32,2688]{1,0:T(8,128)(2,1)S(1)} %shard_map.100), channel_id=1, source_target_pairs={{8,4},{9,5},{10,6},{11,7},{12,0},{13,1},{14,2},{15,3},{16,12},{17,... | collective-permute-start | bytes 516104 | tf_op jit(solution)/shard_map/ppermute | solution.py:329
  33.3 16.3 %collective-permute-start.14 = (bf16[32,2688]{1,0:T(8,128)(2,1)S(1)}, bf16[32,2688]{1,0:T(8,128)(2,1)S(1)}, u32[]{:S(2)}, u32[]{:S(2)}) collective-permute-start(bf16[32,2688]{1,0:T(8,128)(2,1)S(1)} %shard_map.101), channel_id=1, source_target_pairs={{8,6},{9,7},{10,4},{11,5},{12,2},{13,3},{14,0},{15,1},{16,14},{17,... | collective-permute-start | bytes 516104 | tf_op jit(solution)/shard_map/ppermute | solution.py:329
